TPU v7x, 128 devices: a whole 4x4x4 slice. The times are simulated.
128 devices in a mesh: tensor: 4 (over y_hi, core), context: 32 (over z, x, y_lo).
Axes of the slice: x: 4, y: 4 (y_hi: 2, y_lo: 2; y = y_hi * 2 + y_lo), z: 4, core: 2. Of those that a mesh axis runs over, the one named last changes fastest.
Arguments:
- queries: bfloat16 [4096, 8192], P('context', 'tensor'), may hold values from -80 to 80
- keys: bfloat16 [4096, 512], P('context', 'tensor'), may hold values from -4 to 4
- values: bfloat16 [4096, 512], P('context', 'tensor'), may hold values from -48 to 48
- resid: bfloat16 [4096, 4096], P(('context', 'tensor')), may hold values from -3 to 3
- out_weight: bfloat16 [8192, 4096], P('tensor', 'context'), may hold values from -0.0625 to 0.0625
- norm_gain: float32 [4096], replicated, may hold values from 0.1 to 1.9
- routes: int32 [4096, 8], P(('context', 'tensor')), may hold values from 0 to 63, all different within a row; in each aligned block of 32 rows (0 to 31, 32 to 63, ...) at most 6 rows name the same one
- gates: float32 [4096, 8], P(('context', 'tensor')), may hold values from 0.05 to 0.35
- w_gate: bfloat16 [64, 4096, 1536], P('context', None, 'tensor'), may hold values from -0.09375 to 0.09375
- w_up: bfloat16 [64, 4096, 1536], P('context', None, 'tensor'), may hold values from -0.09375 to 0.09375
- w_down: bfloat16 [64, 1536, 4096], P('context', 'tensor'), may hold values from -0.15625 to 0.15625
Outputs:
- mixed: bfloat16 [4096, 4096], P(('context', 'tensor'))
Inputs may be any that keep to these rules, and one draw needn't show every extreme that they name: `routes`: each row names 8 different experts; in each aligned block of 32 rows (the rows of one device) no expert is named by more than 6 rows, a bound that some block reaches.
All inputs are finite; a program needn't handle non-finite values.
Results may differ from a plain program's by a relative error of at most 0.018.
Values may be sent and summed in bfloat16 or wider, within the bound.
A program may use at most 192 MiB of HBM per device.

v0:
```python
import jax
import jax.numpy as jnp
from jax import lax
from jax.sharding import PartitionSpec as P

D = 4096
HEAD_WIDTH = 128
EXP_DEV = 2


def shards(
    queries, keys, values, resid, out_weight, norm_gain, routes, gates, w_gate, w_up, w_down
):
    tok_ctx = queries.shape[0]
    q_local = queries.shape[1] // HEAD_WIDTH
    kv_local = keys.shape[1] // HEAD_WIDTH
    query_group = q_local // kv_local
    n_ctx = lax.axis_size("context")
    first = lax.axis_index("context") * tok_ctx
    scaling = HEAD_WIDTH ** (-0.5)
    grouped = (
        queries.reshape(tok_ctx, kv_local, query_group, HEAD_WIDTH)
        .transpose(1, 2, 0, 3)
        .reshape(kv_local, query_group * tok_ctx, HEAD_WIDTH)
    )
    query_pos = first + jnp.arange(query_group * tok_ctx, dtype=jnp.int32) % tok_ctx
    running = jnp.full((kv_local, query_group * tok_ctx), -1e30, jnp.float32)
    key_part = lax.all_gather(keys, "context", axis=0, tiled=True)
    value_part = lax.all_gather(values, "context", axis=0, tiled=True)
    count = key_part.shape[0]
    key_head_rows = key_part.reshape(count, kv_local, HEAD_WIDTH)
    value_head_rows = value_part.reshape(count, kv_local, HEAD_WIDTH)
    scores = (
        jnp.einsum("gqd,rgd->gqr", grouped, key_head_rows, preferred_element_type=jnp.float32)
        * scaling
    )
    key_pos = jnp.arange(count, dtype=jnp.int32)
    keep = key_pos[None, :] <= query_pos[:, None]
    scores = jnp.where(keep[None, :, :], scores, -jnp.inf)
    newest = jnp.maximum(running, jnp.max(scores, axis=2))
    weights = jnp.exp(scores - newest[:, :, None])
    total = jnp.sum(weights, axis=2)
    summed = jnp.einsum(
        "gqr,rgd->gqd",
        weights.astype(jnp.bfloat16),
        value_head_rows,
        preferred_element_type=jnp.float32,
    )
    running, total, summed = (newest, total, summed)
    heads = (summed / total[:, :, None]).astype(jnp.bfloat16)
    attn = (
        heads.reshape(kv_local, query_group, tok_ctx, HEAD_WIDTH)
        .transpose(2, 0, 1, 3)
        .reshape(tok_ctx, q_local * HEAD_WIDTH)
    )
    partial_out = jnp.dot(
        attn,
        lax.all_gather(out_weight, "context", axis=1, tiled=True),
        preferred_element_type=jnp.float32,
    )
    head_total = lax.psum_scatter(
        partial_out.astype(jnp.bfloat16), "tensor", scatter_dimension=0, tiled=True
    ).astype(jnp.float32)
    hsum = resid.astype(jnp.float32) + head_total
    scale_rows = lax.rsqrt(jnp.mean(hsum * hsum, axis=1, keepdims=True) + 1e-06)
    normed = (hsum * scale_rows * norm_gain).astype(jnp.bfloat16)
    tok_own = resid.shape[0]
    topk = routes.shape[1]
    experts = EXP_DEV * n_ctx
    capacity = max(2, 3 * tok_own * topk // (2 * experts))
    flat = routes.reshape(-1)
    onehot = (flat[:, None] == jnp.arange(experts, dtype=jnp.int32)[None, :]).astype(jnp.int32)
    slots = jnp.sum((jnp.cumsum(onehot, axis=0) - onehot) * onehot, axis=1)
    place = flat * capacity + slots
    outgoing = (
        jnp.zeros((experts * capacity, D), jnp.bfloat16)
        .at[place]
        .set(jnp.repeat(normed, topk, axis=0))
    )
    outgoing = outgoing.reshape(n_ctx, EXP_DEV, capacity, D)
    arrived = lax.all_to_all(outgoing, "context", split_axis=0, concat_axis=0, tiled=True)
    shared = lax.all_gather(arrived, "tensor", axis=0, tiled=True)
    gating = jnp.einsum("sjcd,jdf->sjcf", shared, w_gate, preferred_element_type=jnp.float32)
    upward = jnp.einsum("sjcd,jdf->sjcf", shared, w_up, preferred_element_type=jnp.float32)
    hidden = (jax.nn.silu(gating) * upward).astype(jnp.bfloat16)
    reduced = lax.psum_scatter(
        jnp.einsum("sjcf,jfd->sjcd", hidden, w_down, preferred_element_type=jnp.float32).astype(
            jnp.bfloat16
        ),
        "tensor",
        scatter_dimension=0,
        tiled=True,
    )
    results = lax.all_to_all(reduced, "context", split_axis=0, concat_axis=0, tiled=True)
    picked = results.reshape(experts * capacity, D)[place]
    contrib = jnp.einsum("tk,tkd->td", gates, picked.reshape(tok_own, topk, D).astype(jnp.float32))
    return (hsum + contrib).astype(jnp.bfloat16)


def solution(mesh):
    return jax.shard_map(
        shards,
        mesh=mesh,
        in_specs=(
            P("context", "tensor"),
            P("context", "tensor"),
            P("context", "tensor"),
            P(("context", "tensor"), None),
            P("tensor", "context"),
            P(),
            P(("context", "tensor"), None),
            P(("context", "tensor"), None),
            P("context", None, "tensor"),
            P("context", None, "tensor"),
            P("context", "tensor", None),
        ),
        out_specs=P(("context", "tensor"), None),
        check_vma=False,
    )
```

profile of v0, /device:TPU:0, one launch (start us, length us, event | category | flops | bytes accessed | tf_op | source)
XLA Modules:
  0.0 1131.2 jit_solution(9026001315908954600)
XLA Ops:
  6.5 0.7 all-gather.5.cloned.1.call-update
  7.3 0.0 all-gather.7.cloned.1.call-start
  7.3 0.7 all-gather.7.cloned.1.call-update
  8.0 0.0 all-gather.9.cloned.1.call-start
  8.1 0.7 all-gather.9.cloned.1.call-update
  8.7 0.0 reduce-scatter.3.cloned.1.call-start
  8.8 1.3 copy.37
  10.1 0.3 copy.38
  10.4 152.0 %all-gather.5.cloned.1.call-done = bf16[4096,128]{1,0:T(8,128)(2,1)} async-done(((bf16[128,128]{1,0:T(8,128)(2,1)}), bf16[4096,128]{1,0:T(8,128)(2,1)}) %all-gather.5.cloned.1.call-update) | async-done | bytes 1048592 | tf_op jit(solution)/shard_map/all_gather | solution.py:28
  162.4 15.0 %fusion.2 = (f32[2048]{0:T(1024)S(1)}, f32[2048,4096]{1,0:T(8,128)}) fusion(s32[2048]{0:T(1024)S(1)} %fusion.33, bf16[2048,128]{1,0:T(8,128)(2,1)S(1)} %bitcast.87, bf16[4096,128]{1,0:T(8,128)(2,1)} %all-gather.5.cloned.1.call-done), kind=kOutput, calls=%fused_computation.7 | convolution fusion | flops 2181036032 | bytes 35143680 | tf_op jit(solution)/shard_map/gqd,rgd->gqr/dot_general | solution.py:34
  177.5 15.4 %fusion = f32[2048]{0:T(1024)S(1)} fusion(f32[2048,4096]{1,0:T(8,128)} %get-tuple-element.6, f32[2048]{0:T(1024)S(1)} %broadcast_maximum_fusion, s32[2048]{0:T(1024)S(1)} %fusion.33), kind=kLoop, calls=%fused_computation.5 | loop fusion | flops 41940992 | bytes 33579008 | tf_op jit(solution)/shard_map/reduce_sum | solution.py:42
  192.9 122.3 %all-gather.7.cloned.1.call-done = bf16[4096,128]{1,0:T(8,128)(2,1)} async-done(((bf16[128,128]{1,0:T(8,128)(2,1)}), bf16[4096,128]{1,0:T(8,128)(2,1)}) %all-gather.7.cloned.1.call-update) | async-done | bytes 1048592 | tf_op jit(solution)/shard_map/all_gather | solution.py:29
  315.3 15.1 %fusion.21 = bf16[2048,128]{1,0:T(8,128)(2,1)S(1)} fusion(bf16[4096,128]{1,0:T(8,128)(2,1)} %all-gather.7.cloned.1.call-done, f32[2048,4096]{1,0:T(8,128)} %get-tuple-element.6, f32[2048]{0:T(1024)S(1)} %broadcast_maximum_fusion, s32[2048]{0:T(1024)S(1)} %fusion.33, f32[2048]{0:T(1024)S(1)} %fusion), kind=kOutput, calls=%fused_computation.28 | convolution fusion | flops 2189950976 | bytes 35151872 | tf_op jit(solution)/shard_map/gqr,rgd->gqd/dot_general | solution.py:43
  330.4 0.3 copy.39
  330.7 383.6 %all-gather.9.cloned.1.call-done = bf16[2048,4096]{1,0:T(8,128)(2,1)} async-done(((bf16[2048,128]{1,0:T(8,128)(2,1)}), bf16[2048,4096]{1,0:T(8,128)(2,1)}) %all-gather.9.cloned.1.call-update) | async-done | bytes 16777232 | tf_op jit(solution)/shard_map/all_gather | solution.py:58
  714.3 9.2 convolution_convert_fusion
  723.5 0.0 all-gather.11.cloned.1.call-start
  723.5 0.1 copy.41
  723.6 0.1 eq.31
  723.7 0.1 eq.27
  723.8 1.1 reduce-window.6
  724.9 0.2 slice_reduce_fusion
  725.1 0.1 copy.40
  725.2 0.1 mul.60
  725.3 0.1 fusion.31
  725.4 39.0 %reduce-scatter.3.cloned.1.call-done = bf16[32,4096]{1,0:T(8,128)(2,1)} async-done(((bf16[128,4096]{1,0:T(8,128)(2,1)}), bf16[32,4096]{1,0:T(8,128)(2,1)}) %reduce-scatter.3.cloned.1.call-update) | async-done | bytes 262160 | tf_op jit(solution)/shard_map/reduce_scatter | solution.py:61
  764.4 1.1 multiply_reduce_fusion
  765.5 1.8 multiply_convert_fusion
  767.3 4.8 scatter_custom_fusion
  772.2 2.9 reshape.129
  775.0 5.5 copy.44
  780.5 47.4 %all_to_all.10 = bf16[32,2,6,4096]{3,1,2,0:T(2,128)(2,1)S(1)} all-to-all(bf16[32,2,6,4096]{3,1,2,0:T(2,128)(2,1)S(1)} %copy.44), channel_id=1, replica_groups=mesh['tensor'=4,'context'=32] {'context'}, dimensions={0} | all-to-all | bytes 6291456 | tf_op jit(solution)/shard_map/all_to_all | solution.py:81
  827.9 3.8 copy.45
  831.7 0.0 reduce-scatter.5.cloned.1.call-start
  831.7 83.0 %all-gather.11.cloned.1.call-done = bf16[128,2,6,4096]{3,0,2,1:T(8,128)(2,1)} async-done(((bf16[32,2,6,4096]{3,0,2,1:T(8,128)(2,1)}), bf16[128,2,6,4096]{3,0,2,1:T(8,128)(2,1)}) %all-gather.11.cloned.1.call-update) | async-done | bytes 12582928 | tf_op jit(solution)/shard_map/all_gather | solution.py:82
  914.8 12.4 %fusion.6 = f32[2,128,6,384]{3,1,2,0:T(8,128)S(1)} fusion(bf16[128,2,6,4096]{3,0,2,1:T(8,128)(2,1)} %all-gather.11.cloned.1.call-done, bf16[2,4096,384]{2,1,0:T(8,128)(2,1)} %param.20), kind=kOutput, calls=%fused_computation.11 | convolution fusion | flops 4831838208 | bytes 21233664 | tf_op jit(solution)/shard_map/sjcd,jdf->sjcf/dot_general | solution.py:84
  927.2 9.2 fusion.10
  936.4 9.6 convert_bitcast_fusion
  946.0 105.5 %reduce-scatter.5.cloned.1.call-done = bf16[32,2,6,4096]{3,0,2,1:T(8,128)(2,1)} async-done(((bf16[128,2,6,4096]{3,0,2,1:T(8,128)(2,1)}), bf16[32,2,6,4096]{3,0,2,1:T(8,128)(2,1)}) %reduce-scatter.5.cloned.1.call-update) | async-done | bytes 3145744 | tf_op jit(solution)/shard_map/reduce_scatter | solution.py:86
  1051.6 6.8 copy.46
  1058.4 7.5 all-to-all-start.1
  1065.9 0.1 copy.51
  1066.0 42.2 %all-to-all-done.1 = bf16[32,2,6,4096]{3,1,2,0:T(2,128)(2,1)S(1)} async-done(((bf16[32,2,6,4096]{3,1,2,0:T(2,128)(2,1)}), bf16[32,2,6,4096]{3,1,2,0:T(2,128)(2,1)S(1)}, u32[]{:S(2)}, u32[]{:S(2)}) %all-to-all-start.1) | async-done | bytes 3145760 | tf_op jit(solution)/shard_map/all_to_all | solution.py:94
  1108.2 4.3 copy.47
  1112.5 4.2 reshape.130
  1116.6 3.2 gather_fusion
  1119.8 2.3 fusion.14
  1122.1 2.0 fusion.28
  (28 shorter events, 0.2 us)
Async XLA Ops:
  6.5 155.9 %all-gather.5.cloned.1.call-start = ((), (), s32[]{:S(2)}) async-start(), calls=%async_computation.4 | async-start | bytes 1081344 | tf_op jit(solution)/shard_map/all_gather | solution.py:28
  7.3 308.0 %all-gather.7.cloned.1.call-start = ((), (), s32[]{:S(2)}) async-start(), calls=%async_computation.5 | async-start | bytes 1081344 | tf_op jit(solution)/shard_map/all_gather | solution.py:29
  8.0 706.3 %all-gather.9.cloned.1.call-start = ((), (), s32[]{:S(2)}) async-start(), calls=%async_computation.6 | async-start | bytes 17301504 | tf_op jit(solution)/shard_map/all_gather | solution.py:58
  8.7 755.6 %reduce-scatter.3.cloned.1.call-start = ((), (), s32[]{:S(2)}) async-start(), calls=%async_computation.7 | async-start | bytes 1310720 | tf_op jit(solution)/shard_map/reduce_scatter | solution.py:61
  714.3 9.2 copy-start.2
  714.3 50.1 %copy-start = (bf16[32,4096]{1,0:T(8,128)(2,1)S(1)}, bf16[32,4096]{1,0:T(8,128)(2,1)}, u32[]{:S(2)}) copy-start(bf16[32,4096]{1,0:T(8,128)(2,1)} %param.14) | copy-start | bytes 786436
  714.3 51.2 %copy-start.1 = (f32[4096]{0:T(1024)S(1)}, f32[4096]{0:T(1024)}, u32[]{:S(2)}) copy-start(f32[4096]{0:T(1024)} %param.16) | copy-start | bytes 49156
  723.5 191.3 %all-gather.11.cloned.1.call-start = ((), (), s32[]{:S(2)}) async-start(), calls=%async_computation.8 | async-start | bytes 15728640 | tf_op jit(solution)/shard_map/all_gather | solution.py:82
  831.7 219.9 %reduce-scatter.5.cloned.1.call-start = ((), (), s32[]{:S(2)}) async-start(), calls=%async_computation.9 | async-start | bytes 15728640 | tf_op jit(solution)/shard_map/reduce_scatter | solution.py:86
  914.8 12.4 %copy-start.4 = (bf16[128,2,6,4096]{3,0,2,1:T(8,128)(2,1)S(1)}, bf16[128,2,6,4096]{3,0,2,1:T(8,128)(2,1)}, u32[]{:S(2)}) copy-start(bf16[128,2,6,4096]{3,0,2,1:T(8,128)(2,1)} %all-gather.11.cloned.1.call-done) | copy-start | bytes 37748740
  914.8 21.6 %slice-start = ((s8[6291456]{0:T(1024)(128)(4,1)}), s8[4194304]{0:T(1024)(128)(4,1)S(1)}, s32[]{:S(2)}) async-start(s8[6291456]{0:T(1024)(128)(4,1)} %bitcast.93), calls=%async_computation.10 | async-start | bytes 8388608
  927.2 9.2 slice-start.1
  946.0 119.9 %copy-start.3 = (f32[32,8]{0,1:T(8,128)S(1)}, f32[32,8]{0,1:T(8,128)}, u32[]{:S(2)}) copy-start(f32[32,8]{0,1:T(8,128)} %param.18) | copy-start | bytes 3076
  1058.4 49.8 %all-to-all-start.1 = ((bf16[32,2,6,4096]{3,1,2,0:T(2,128)(2,1)}), bf16[32,2,6,4096]{3,1,2,0:T(2,128)(2,1)S(1)}, u32[]{:S(2)}, u32[]{:S(2)}) async-start(bf16[32,2,6,4096]{3,1,2,0:T(2,128)(2,1)} %copy.46), calls=%async_computation.3 | async-start | bytes 6291456 | tf_op jit(solution)/shard_map/all_to_all | solution.py:94
Sparse Core Ops, SparseCore 0:
  9.0 153.3 all-gather.4
  164.1 151.1 all-gather.6
  316.8 397.4 all-gather.8
  723.6 40.7 reduce-scatter.2
  831.8 82.9 all-gather.10
  946.1 105.3 reduce-scatter.4
where the time goes:
time: 1140 us; the launch traced here: 1130 us
  waiting for transfers between devices  930 us (82%)
  matrix products  72.8 us (6%)
  blocking collectives  47.4 us (4%)
  local copies, waits for them, and re-layouts  38 us (3%)
  other arithmetic  21.6 us (2%)
  between operations  13.9 us (1%)
    all_gather x1, waiting for transfers between devices, shards(): lax.all_gather(out_weight, 'context', axis=1, tiled=True)  384 us
    all_gather x1, waiting for transfers between devices, shards(): key_part = lax.all_gather(keys, 'context', axis=0, tiled=True)  152 us
    all_gather x1, waiting for transfers between devices, shards(): value_part = lax.all_gather(values, 'context', axis=0, tiled=True)  122 us
    reduce_scatter x1, waiting for transfers between devices, shards(): lax.psum_scatter(jnp.einsum('sjcf,jfd->sjcd', hidden, w_down, preferred_e...  106 us
    all_gather x1, waiting for transfers between devices, shards(): shared = lax.all_gather(arrived, 'tensor', axis=0, tiled=True)  83 us
    all_to_all x1, blocking collectives, shards(): lax.all_to_all(outgoing, 'context', split_axis=0, concat_axis=0, tiled=True)  47.4 us
    all_to_all x1, waiting for transfers between devices, shards(): lax.all_to_all(reduced, 'context', split_axis=0, concat_axis=0, tiled=True)  42.2 us
    reduce_scatter x1, waiting for transfers between devices, shards(): lax.psum_scatter(partial_out.astype(jnp.bfloat16), 'tensor', scatter_dime...  39 us
  transfers between devices with their start and end apart: 7, of which 7 were waited for; matrix products, arithmetic and copies ran while one was open for 4% of the time, Pallas kernels for 0%

commit v1 on v0

v1 whole, which is shorter than its diff:
```python
import functools
import jax
import jax.numpy as jnp
from jax import lax
from jax.experimental import pallas as pl
from jax.experimental.pallas import tpu as pltpu
from jax.sharding import PartitionSpec as P

D = 4096
HW = 128
MESH = pl.DeviceIdType.MESH
BF = jnp.bfloat16
F32 = jnp.float32


def place():
    c = lax.axis_index("context")
    t = lax.axis_index("tensor")
    return c // 8, (c // 2) % 4, c % 2, t // 2, t % 2


def device(z, x, yl, yh, core):
    return {"context": z * 8 + x * 2 + yl, "tensor": yh * 2 + core}


def send(src, dst, ssem, rsem, to):
    copy = pltpu.make_async_remote_copy(
        src_ref=src, dst_ref=dst, send_sem=ssem, recv_sem=rsem, device_id=to, device_id_type=MESH
    )
    copy.start()
    return copy


def greet(peers):
    barrier = pltpu.get_barrier_semaphore()
    for peer in peers:
        pl.semaphore_signal(barrier, inc=1, device_id=peer, device_id_type=MESH)
    pl.semaphore_wait(barrier, len(peers))


def attention_kernel(
    q_ref, k_ref, v_ref, w_ref, resid_ref, gain_ref, hsum_ref, normed_ref,
    kall, vall, wall, att, scores, acc, sib_out, sib_in, own_out, own_in,
    k_s, k_r, v_s, v_r, w_s, w_r, a_s, a_r, c_s, c_r, o_s, o_r,
):
    z, x, yl, yh, core = place()
    ctx = z * 8 + x * 2 + yl
    zs = [lax.rem(z + o, 4) for o in range(4)]
    xs = [lax.rem(x + o, 4) for o in range(4)]
    group = [(o, p) for o in range(4) for p in range(2)][1:]
    sibling = device(z, x, yl, yh, 1 - core)
    z_peers = [device(zs[o], x, yl, yh, core) for o in (1, 2, 3)]
    x_peers = [device(z, xs[o], yl, yh, core) for o in (1, 2, 3)]
    y_peer = device(z, x, 1 - yl, yh, core)
    w_peers = [device(z, xs[o], lax.rem(yl + p, 2), yh, core) for o, p in group]
    o_peers = [device(zs[o], x, yl, lax.rem(yh + p, 2), core) for o, p in group]
    greet([sibling] + z_peers + w_peers + [device(zs[o], x, yl, 1 - yh, core) for o in range(4)])

    kall[z, x, yl] = k_ref[...]
    vall[z, x, yl] = v_ref[...]
    me = (z, x, yl)
    k1 = [send(kall.at[me], kall.at[me], k_s.at[i], k_r.at[i], z_peers[i]) for i in range(3)]
    v1 = [send(vall.at[me], vall.at[me], v_s.at[0], v_r.at[0], y_peer)]
    for copy in v1 + k1:
        copy.wait_recv()
    k2 = [
        send(kall.at[:, x, yl], kall.at[:, x, yl], k_s.at[3 + i], k_r.at[3 + i], x_peers[i])
        for i in range(3)
    ]
    v2 = [
        send(vall.at[z, x], vall.at[z, x], v_s.at[1 + i], v_r.at[1 + i], x_peers[i])
        for i in range(3)
    ]
    for copy in v2 + k2:
        copy.wait_recv()
    k3 = [send(kall.at[:, :, yl], kall.at[:, :, yl], k_s.at[6], k_r.at[6], y_peer)]
    v3 = [send(vall.at[z], vall.at[z], v_s.at[4 + i], v_r.at[4 + i], z_peers[i]) for i in range(3)]
    mine = pl.ds(pl.multiple_of((x * 2 + yl) * 128, 128), 128)
    wcopies = [
        send(w_ref, wall.at[:, mine], w_s.at[i], w_r.at[i], w_peers[i]) for i in range(7)
    ]
    wall[:, mine] = w_ref[...]
    for copy in v3 + k3:
        copy.wait_recv()

    factor = HW**-0.5 * 1.4426950408889634
    last = ctx // 4
    nrow = 512

    def keys_of(ref, ch):
        return ref[ch // 2, pl.ds((ch % 2) * 2, 2)].reshape(512, HW)

    def columns(ch):
        return pl.ds(pl.multiple_of(ch * 512, 512), 512)

    def fold(f, s):
        return f(f(s[:, 0:128], s[:, 128:256]), f(s[:, 256:384], s[:, 384:512]))

    def heads(hc, carry):
        q = jnp.concatenate(
            [
                q_ref[:, pl.ds(pl.multiple_of(hc * 512 + i * HW, HW), HW)]
                for i in range(4)
            ],
            axis=0,
        )

        def product(ch):
            return lax.dot_general(
                q, keys_of(kall, ch), (((1,), (1,)), ((), ())), preferred_element_type=F32
            )

        def first(ch, top):
            s = product(ch)
            scores[:, columns(ch)] = s
            return jnp.maximum(top, fold(jnp.maximum, s))

        top = lax.fori_loop(0, last, first, jnp.full((nrow, 128), -jnp.inf, F32))
        s = product(last)
        row = lax.broadcasted_iota(jnp.int32, (nrow, 512), 0) % 128
        col = lax.broadcasted_iota(jnp.int32, (nrow, 512), 1)
        s = jnp.where(col <= row + (ctx % 4) * 128, s, -jnp.inf)
        scores[:, columns(last)] = s
        top = jnp.maximum(top, fold(jnp.maximum, s))
        shift = jnp.max(top, axis=1, keepdims=True) * factor

        def second(ch, carry):
            total, summed = carry
            p = jnp.exp2(scores[:, columns(ch)] * factor - shift)
            total = total + fold(jnp.add, p)
            summed = summed + jnp.dot(p.astype(BF), keys_of(vall, ch), preferred_element_type=F32)
            return total, summed

        zero = jnp.zeros((nrow, 128), F32)
        total, summed = lax.fori_loop(0, last + 1, second, (zero, zero))
        out = (summed / jnp.sum(total, axis=1, keepdims=True)).astype(BF)
        for i in range(4):
            att[z, hc, :, i * HW : (i + 1) * HW] = out[i * 128 : (i + 1) * 128]
        for i in range(3):
            send(att.at[z, hc], att.at[z, hc], a_s.at[hc, i], a_r.at[hc, i], z_peers[i])
        return carry

    lax.fori_loop(0, 4, heads, 0)
    for copy in wcopies:
        copy.wait_recv()

    def project(hc, carry):
        for i in range(3):
            pltpu.make_async_remote_copy(
                src_ref=att.at[z, hc], dst_ref=att.at[z, hc], send_sem=a_s.at[hc, i],
                recv_sem=a_r.at[hc, i], device_id=z_peers[i], device_id_type=MESH,
            ).wait()
        a = att[:, hc].reshape(512, 512)
        for n in range(4):
            cols = slice(n * 256, (n + 1) * 256)
            r = jnp.dot(
                a, wall[pl.ds(pl.multiple_of(hc * 512, 512), 512), cols], preferred_element_type=F32
            ).reshape(4, 2, 2, 32, 256)
            acc[:, :, :, :, cols] = jnp.where(hc == 0, r, acc[:, :, :, :, cols] + r)
        return carry

    acc[...] = jnp.zeros_like(acc)
    lax.fori_loop(0, 4, project, 0)
    sib_out[...] = acc[:, :, 1 - core].astype(BF)
    copy = send(sib_out, sib_in, c_s.at[0], c_r.at[0], sibling)
    copy.wait()
    own_out[...] = (acc[:, :, core] + sib_in[...].astype(F32)).astype(BF)
    ocopies = []
    for i, (o, p) in enumerate(group):
        ocopies.append(
            send(
                own_out.at[zs[o], lax.rem(yh + p, 2)], own_in.at[z, yh], o_s.at[i], o_r.at[i], o_peers[i]
            )
        )
    own_in[z, yh] = own_out[z, yh]
    for copy in ocopies:
        copy.wait()
    square = jnp.zeros((32, 1), F32)
    for n in range(4):
        h = resid_ref[:, n * 1024 : (n + 1) * 1024].astype(F32) + (
            own_in[n, 0].astype(F32) + own_in[n, 1].astype(F32)
        )
        hsum_ref[n] = h
        square = square + jnp.sum(h * h, axis=1, keepdims=True)
    scale = lax.rsqrt(square * (1.0 / D) + 1e-06)
    for n in range(4):
        normed_ref[n] = (hsum_ref[n] * scale * gain_ref[:, n * 1024 : (n + 1) * 1024]).astype(BF)
    for copy in k1 + k2 + k3 + v1 + v2 + v3 + wcopies:
        copy.wait_send()


def attention(queries, keys, values, out_weight, resid, norm_gain):
    dma = pltpu.SemaphoreType.DMA
    vm = pl.BlockSpec(memory_space=pltpu.VMEM)
    return pl.pallas_call(
        attention_kernel,
        out_shape=(
            jax.ShapeDtypeStruct((4, 32, 1024), F32),
            jax.ShapeDtypeStruct((4, 32, 1024), BF),
        ),
        in_specs=[vm] * 6,
        out_specs=(vm, vm),
        scratch_shapes=[
            pltpu.VMEM((4, 4, 2, 128, 128), BF),
            pltpu.VMEM((4, 4, 2, 128, 128), BF),
            pltpu.VMEM((2048, 1024), BF),
            pltpu.VMEM((4, 4, 128, 512), BF),
            pltpu.VMEM((512, 4096), F32),
            pltpu.VMEM((4, 2, 2, 32, 1024), F32),
            pltpu.VMEM((4, 2, 32, 1024), BF),
            pltpu.VMEM((4, 2, 32, 1024), BF),
            pltpu.VMEM((4, 2, 32, 1024), BF),
            pltpu.VMEM((4, 2, 32, 1024), BF),
            dma((7,)), dma((7,)), dma((7,)), dma((7,)), dma((7,)), dma((7,)),
            dma((4, 3)), dma((4, 3)), dma((1,)), dma((1,)), dma((7,)), dma((7,)),
        ],
        compiler_params=pltpu.CompilerParams(
            collective_id=0, has_side_effects=True, vmem_limit_bytes=56 * 2**20
        ),
        cost_estimate=pl.CostEstimate(flops=8 * 10**9, bytes_accessed=4 * 2**20, transcendentals=8 * 2**20),
    )(queries, keys, values, out_weight, resid, norm_gain.reshape(1, D))


EXP_DEV = 2


def shards(
    queries, keys, values, resid, out_weight, norm_gain, routes, gates, w_gate, w_up, w_down
):
    n_ctx = lax.axis_size("context")
    hsum, normed = attention(queries, keys, values, out_weight, resid, norm_gain)
    hsum = hsum.transpose(1, 0, 2).reshape(32, D)
    normed = normed.transpose(1, 0, 2).reshape(32, D)
    tok_own = resid.shape[0]
    topk = routes.shape[1]
    experts = EXP_DEV * n_ctx
    capacity = max(2, 3 * tok_own * topk // (2 * experts))
    flat = routes.reshape(-1)
    onehot = (flat[:, None] == jnp.arange(experts, dtype=jnp.int32)[None, :]).astype(jnp.int32)
    slots = jnp.sum((jnp.cumsum(onehot, axis=0) - onehot) * onehot, axis=1)
    place = flat * capacity + slots
    outgoing = (
        jnp.zeros((experts * capacity, D), jnp.bfloat16)
        .at[place]
        .set(jnp.repeat(normed, topk, axis=0))
    )
    outgoing = outgoing.reshape(n_ctx, EXP_DEV, capacity, D)
    arrived = lax.all_to_all(outgoing, "context", split_axis=0, concat_axis=0, tiled=True)
    shared = lax.all_gather(arrived, "tensor", axis=0, tiled=True)
    gating = jnp.einsum("sjcd,jdf->sjcf", shared, w_gate, preferred_element_type=jnp.float32)
    upward = jnp.einsum("sjcd,jdf->sjcf", shared, w_up, preferred_element_type=jnp.float32)
    hidden = (jax.nn.silu(gating) * upward).astype(jnp.bfloat16)
    reduced = lax.psum_scatter(
        jnp.einsum("sjcf,jfd->sjcd", hidden, w_down, preferred_element_type=jnp.float32).astype(
            jnp.bfloat16
        ),
        "tensor",
        scatter_dimension=0,
        tiled=True,
    )
    results = lax.all_to_all(reduced, "context", split_axis=0, concat_axis=0, tiled=True)
    picked = results.reshape(experts * capacity, D)[place]
    contrib = jnp.einsum("tk,tkd->td", gates, picked.reshape(tok_own, topk, D).astype(jnp.float32))
    return (hsum + contrib).astype(jnp.bfloat16)


def solution(mesh):
    return jax.shard_map(
        shards,
        mesh=mesh,
        in_specs=(
            P("context", "tensor"),
            P("context", "tensor"),
            P("context", "tensor"),
            P(("context", "tensor"), None),
            P("tensor", "context"),
            P(),
            P(("context", "tensor"), None),
            P(("context", "tensor"), None),
            P("context", None, "tensor"),
            P("context", None, "tensor"),
            P("context", "tensor", None),
        ),
        out_specs=P(("context", "tensor"), None),
        check_vma=False,
    )
```

time: 1140 us -> 483 us (0.42)
  waiting for transfers between devices: 930 us -> 230 us
  Pallas kernels: 0 us -> 97.1 us
  matrix products: 72.8 us -> 33.3 us
  other arithmetic: 21.6 us -> 3.53 us
    all_gather x3 -> x0, waiting for transfers between devices: 658 us -> none  [the longest x1 384 us: shards(): lax.all_gather(out_weight, 'context', axis=1, tiled=True)]
    pallas_call x0 -> x1, Pallas kernels: none -> 97.1 us  [attention(): pl.pallas_call(attention_kernel, out_shape=(jax.ShapeDtypeStruct((4, 32,...]
    dot_general x3 -> x0, matrix products: 39.3 us -> none  [the longest x1 15.1 us: shards(): jnp.einsum('gqr,rgd->gqd', weights.astype(jnp.bfloat16), value_head_rows,...]
    reduce_scatter x1 -> x0, waiting for transfers between devices: 39 us -> none  [shards(): lax.psum_scatter(partial_out.astype(jnp.bfloat16), 'tensor', scatter_dime...]
    reduce_sum x2 -> x0, other arithmetic: 16.6 us -> none  [the longest x1 15.4 us: shards(): total = jnp.sum(weights, axis=2)]
  transfers between devices with their start and end apart: 7 -> 3, of which waited for: 7 -> 3; matrix products, arithmetic and copies ran while one was open for 4% -> 0% of each run, Pallas kernels for 0% -> 0%
where the time goes in v1:
time: 483 us
  waiting for transfers between devices  230 us (48%)
  Pallas kernels  97.1 us (20%)
  blocking collectives  58.7 us (12%)
  local copies, waits for them, and re-layouts  39.3 us (8%)
  matrix products  33.3 us (7%)
  between operations  13.5 us (3%)
  starting transfers between devices  7.65 us (2%)
    reduce_scatter x1, waiting for transfers between devices, shards(): lax.psum_scatter(jnp.einsum('sjcf,jfd->sjcd', hidden, w_down, preferred_e...  106 us
    pallas_call x1, Pallas kernels, attention(): pl.pallas_call(attention_kernel, out_shape=(jax.ShapeDtypeStruct((4, 32,...  97.1 us
    all_gather x1, waiting for transfers between devices, shards(): shared = lax.all_gather(arrived, 'tensor', axis=0, tiled=True)  83.9 us
    all_to_all x1, blocking collectives, shards(): lax.all_to_all(outgoing, 'context', split_axis=0, concat_axis=0, tiled=True)  58.7 us
    all_to_all x1, waiting for transfers between devices, shards(): lax.all_to_all(reduced, 'context', split_axis=0, concat_axis=0, tiled=True)  40.1 us
    dot_general x1, matrix products, shards(): jnp.einsum('sjcd,jdf->sjcf', shared, w_up, preferred_element_type=jnp.flo...  12.3 us
  transfers between devices with their start and end apart: 3, of which 3 were waited for; matrix products, arithmetic and copies ran while one was open for 0% of the time, Pallas kernels for 0%

profile of v1, /device:TPU:0, one launch (start us, length us, event | category | flops | bytes accessed | tf_op | source)
XLA Modules:
  0.0 482.7 jit_solution(9980928718213413195)
XLA Ops:
  6.5 0.0 all-gather.2.cloned.1.call-start
  6.5 0.8 copy.30
  7.3 0.1 eq.29
  7.4 0.1 eq.25
  7.5 0.7 broadcast_multiply_fusion
  8.2 0.6 reduce-window.6
  8.8 0.2 slice_reduce_fusion
  9.0 0.1 copy.29
  9.1 0.1 mul.28
  9.2 97.1 %shard_map.109 = (f32[4,32,1024]{2,1,0:T(8,128)}, bf16[4,32,1024]{2,1,0:T(8,128)(2,1)}) custom-call(bf16[128,2048]{1,0:T(8,128)(2,1)} %q_ref.1, bf16[128,128]{1,0:T(8,128)(2,1)} %k_ref.1, bf16[128,128]{1,0:T(8,128)(2,1)} %v_ref.1, bf16[2048,128]{1,0:T(8,128)(2,1)} %w_ref.1, bf16[32,4096]{1,0:T(8,128)(2,1)} %resid_ref.1, f32[1,4096]{1,0:T(1,128)} %bitcast.89), custom_call_target="tpu_custom_call" | custom-call | flops 8000000000 | bytes 4194304 | tf_op jit(solution)/shard_map/pallas_call | solution.py:195
  106.3 1.0 copy.45
  107.3 0.1 fusion.20
  107.4 4.4 scatter_custom_fusion
  111.8 2.9 reshape.72
  114.7 5.5 %copy.34 = bf16[32,2,6,4096]{3,1,2,0:T(2,128)(2,1)S(1)} copy(bf16[32,2,6,4096]{3,2,1,0:T(8,128)(2,1)} %reshape.72) | data formatting | bytes 6291456 | tf_op jit(solution)/shard_map/reshape | solution.py:247
  120.2 58.7 %all_to_all.10 = bf16[32,2,6,4096]{3,1,2,0:T(2,128)(2,1)S(1)} all-to-all(bf16[32,2,6,4096]{3,1,2,0:T(2,128)(2,1)S(1)} %copy.34), channel_id=1, replica_groups=mesh['tensor'=4,'context'=32] {'context'}, dimensions={0} | all-to-all | bytes 6291456 | tf_op jit(solution)/shard_map/all_to_all | solution.py:248
  178.9 3.8 copy.35
  182.7 0.0 all-gather.2.cloned.1.call-update
  182.7 0.0 reduce-scatter.2.cloned.1.call-start
  182.8 83.9 %all-gather.2.cloned.1.call-done = bf16[128,2,6,4096]{3,0,2,1:T(8,128)(2,1)} async-done(((bf16[32,2,6,4096]{3,0,2,1:T(8,128)(2,1)}), bf16[128,2,6,4096]{3,0,2,1:T(8,128)(2,1)}) %all-gather.2.cloned.1.call-update) | async-done | bytes 12582928 | tf_op jit(solution)/shard_map/all_gather | solution.py:249
  266.7 0.0 copy-start.1
  266.7 0.0 slice-start
  266.7 12.3 %fusion.1 = f32[2,128,6,384]{3,1,2,0:T(8,128)S(1)} fusion(bf16[128,2,6,4096]{3,0,2,1:T(8,128)(2,1)} %all-gather.2.cloned.1.call-done, bf16[2,4096,384]{2,1,0:T(8,128)(2,1)} %param.20), kind=kOutput, calls=%fused_computation.4 | convolution fusion | flops 4831838208 | bytes 21233664 | tf_op jit(solution)/shard_map/sjcd,jdf->sjcf/dot_general | solution.py:251
  279.0 0.0 copy-done.1
  279.0 0.0 slice-start.1
  279.0 9.2 %fusion.5 = bf16[128,2,6,384]{3,0,2,1:T(8,128)(2,1)S(1)} fusion(f32[2,128,6,384]{3,1,2,0:T(8,128)S(1)} %fusion.1, bf16[128,2,6,4096]{3,0,2,1:T(8,128)(2,1)S(1)} %copy-done.1, bf16[2,4096,384]{2,1,0:T(8,128)(2,1)} %param.19), kind=kOutput, calls=%fused_computation.9 | convolution fusion | flops 4835377152 | bytes 22413312 | tf_op jit(solution)/shard_map/sjcd,jdf->sjcf/dot_general | solution.py:250
  288.2 0.0 slice-done
  288.2 0.0 slice-done.1
  288.2 9.5 %convert_bitcast_fusion = bf16[128,2,6,4096]{3,0,2,1:T(8,128)(2,1)} fusion(bf16[128,2,6,384]{3,0,2,1:T(8,128)(2,1)S(1)} %fusion.5, bf16[2,384,4096]{2,1,0:T(8,128)(2,1)S(1)} %bitcast.88), kind=kOutput, calls=%fused_computation.2 | convolution fusion | flops 4838129664 | bytes 20054016 | tf_op jit(solution)/shard_map/sjcf,jfd->sjcd/dot_general | solution.py:254
  297.7 0.0 reduce-scatter.2.cloned.1.call-update
  297.8 105.6 %reduce-scatter.2.cloned.1.call-done = bf16[32,2,6,4096]{3,0,2,1:T(8,128)(2,1)} async-done(((bf16[128,2,6,4096]{3,0,2,1:T(8,128)(2,1)}), bf16[32,2,6,4096]{3,0,2,1:T(8,128)(2,1)}) %reduce-scatter.2.cloned.1.call-update) | async-done | bytes 3145744 | tf_op jit(solution)/shard_map/reduce_scatter | solution.py:253
  403.3 6.8 %copy.36 = bf16[32,2,6,4096]{3,1,2,0:T(2,128)(2,1)} copy(bf16[32,2,6,4096]{3,0,2,1:T(8,128)(2,1)} %reduce-scatter.2.cloned.1.call-done) | data formatting | bytes 6291456 | tf_op jit(solution)/shard_map/reduce_scatter | solution.py:253
  410.1 0.0 copy-start
  410.1 7.6 %all-to-all-start.1 = ((bf16[32,2,6,4096]{3,1,2,0:T(2,128)(2,1)}), bf16[32,2,6,4096]{3,1,2,0:T(2,128)(2,1)S(1)}, u32[]{:S(2)}, u32[]{:S(2)}) async-start(bf16[32,2,6,4096]{3,1,2,0:T(2,128)(2,1)} %copy.36), calls=%async_computation.2 | async-start | bytes 6291456 | tf_op jit(solution)/shard_map/all_to_all | solution.py:261
  417.8 0.0 copy-done
  417.8 0.1 copy.41
  417.9 1.9 copy.43
  419.8 40.1 %all-to-all-done.1 = bf16[32,2,6,4096]{3,1,2,0:T(2,128)(2,1)S(1)} async-done(((bf16[32,2,6,4096]{3,1,2,0:T(2,128)(2,1)}), bf16[32,2,6,4096]{3,1,2,0:T(2,128)(2,1)S(1)}, u32[]{:S(2)}, u32[]{:S(2)}) %all-to-all-start.1) | async-done | bytes 3145760 | tf_op jit(solution)/shard_map/all_to_all | solution.py:261
  459.8 4.3 copy.37
  464.1 4.2 reshape.73
  468.3 3.2 gather_fusion
  471.5 2.3 fusion.9
  473.7 2.1 fusion.17
  (6 shorter events, 0.1 us)
Async XLA Ops:
  6.5 260.1 %all-gather.2.cloned.1.call-start = ((), (), s32[]{:S(2)}) async-start(), calls=%async_computation.3 | async-start | bytes 15728640 | tf_op jit(solution)/shard_map/all_gather | solution.py:249
  182.7 220.6 %reduce-scatter.2.cloned.1.call-start = ((), (), s32[]{:S(2)}) async-start(), calls=%async_computation.4 | async-start | bytes 15728640 | tf_op jit(solution)/shard_map/reduce_scatter | solution.py:253
  266.7 12.3 %copy-start.1 = (bf16[128,2,6,4096]{3,0,2,1:T(8,128)(2,1)S(1)}, bf16[128,2,6,4096]{3,0,2,1:T(8,128)(2,1)}, u32[]{:S(2)}) copy-start(bf16[128,2,6,4096]{3,0,2,1:T(8,128)(2,1)} %all-gather.2.cloned.1.call-done) | copy-start | bytes 37748740
  266.7 21.5 %slice-start = ((s8[6291456]{0:T(1024)(128)(4,1)}), s8[4194304]{0:T(1024)(128)(4,1)S(1)}, s32[]{:S(2)}) async-start(s8[6291456]{0:T(1024)(128)(4,1)} %bitcast.87), calls=%async_computation.5 | async-start | bytes 8388608
  279.0 9.2 %slice-start.1 = ((s8[6291456]{0:T(1024)(128)(4,1)}), s8[2097152]{0:T(1024)(128)(4,1)S(1)}, s32[]{:S(2)}) async-start(s8[6291456]{0:T(1024)(128)(4,1)} %bitcast.87), calls=%async_computation.6 | async-start | bytes 4194304
  410.1 7.6 %copy-start = (f32[32,8]{0,1:T(8,128)S(1)}, f32[32,8]{0,1:T(8,128)}, u32[]{:S(2)}) copy-start(f32[32,8]{0,1:T(8,128)} %param.18) | copy-start | bytes 3076
  410.1 49.7 %all-to-all-start.1 = ((bf16[32,2,6,4096]{3,1,2,0:T(2,128)(2,1)}), bf16[32,2,6,4096]{3,1,2,0:T(2,128)(2,1)S(1)}, u32[]{:S(2)}, u32[]{:S(2)}) async-start(bf16[32,2,6,4096]{3,1,2,0:T(2,128)(2,1)} %copy.36), calls=%async_computation.2 | async-start | bytes 6291456 | tf_op jit(solution)/shard_map/all_to_all | solution.py:261
Sparse Core Ops, SparseCore 0:
  182.9 83.7 all-gather.1
  297.9 105.3 reduce-scatter.1

commit v2 on v1

--- a/solution.py
+++ b/solution.py
@@ -221,47 +221,411 @@
     )(queries, keys, values, out_weight, resid, norm_gain.reshape(1, D))
 
 
-EXP_DEV = 2
+CH = 4
+CW = D // CH
+
+
+def experts_kernel(
+    normed_ref, hsum_ref, routes_ref, gates_ref, wg_ref, wu_ref, wd_ref, out_ref,
+    tok, meta, stage, rows, acc, hid, wgu, wdn, back, zin, uin, vout, vin, pick, give,
+    m_s, m_r, s1_s, s1_r, s2_s, s2_r, s3_s, s3_r, s4_s, s4_r,
+    y_s, y_r, b3_s, b3_r, b2_s, b2_r, b1_s, b1_r, wg_m, wu_m, wd_m,
+):
+    z, x, yl, yh, core = place()
+    y = yh * 2 + yl
+    a = z * (1 - core) + x * core
+    c = x * (1 - core) + z * core
+
+    def at(a_, y_, c_):
+        return device(
+            a_ * (1 - core) + c_ * core, c_ * (1 - core) + a_ * core, y_ % 2, y_ // 2, core
+        )
+
+    As = [lax.rem(a + o, 4) for o in range(4)]
+    Ys = [lax.rem(y + o, 4) for o in range(4)]
+    Cs = [lax.rem(c + o, 4) for o in range(4)]
+    a_peers = [at(As[o], y, c) for o in (1, 2, 3)]
+    y_peers = [at(a, Ys[o], c) for o in (1, 2, 3)]
+    c_peers = [at(a, y, Cs[o]) for o in (1, 2, 3)]
+    sibling = device(z, x, yl, yh, 1 - core)
+    greet([sibling] + a_peers + y_peers + c_peers)
+
+    def remote(src, dst, ssem, rsem, to):
+        return pltpu.make_async_remote_copy(
+            src_ref=src, dst_ref=dst, send_sem=ssem, recv_sem=rsem, device_id=to, device_id_type=MESH
+        )
+
+    def m1(i):
+        return remote(meta.at[y, a], meta.at[y, a], m_s.at[i], m_r.at[i], a_peers[i])
+
+    def m2(i):
+        return remote(meta.at[y], meta.at[y], m_s.at[3 + i], m_r.at[3 + i], y_peers[i])
+
+    def s1(q, i):
+        return remote(normed_ref.at[q], tok.at[q, y, a], s1_s.at[q, i], s1_r.at[q, i], a_peers[i])
+
+    def s2(q, i):
+        return remote(tok.at[q, y], tok.at[q, y], s2_s.at[q, i], s2_r.at[q, i], y_peers[i])
+
+    def s3(q, i):
+        return remote(
+            stage.at[q, i], rows.at[q, 0, :, c], s3_s.at[q, i], s3_r.at[q, i], c_peers[i]
+        )
+
+    def s4(q):
+        return remote(rows.at[q, 0], rows.at[q, 1], s4_s.at[q], s4_r.at[q], sibling)
+
+    def yb(q):
+        return remote(rows.at[q, 1], back.at[q], y_s.at[q], y_r.at[q], sibling)
+
+    def b3(q, i):
+        return remote(
+            rows.at[q, 0, :, Cs[i + 1]], zin.at[q, c], b3_s.at[q, i], b3_r.at[q, i], c_peers[i]
+        )
+
+    def b2(q, i):
+        return remote(tok.at[q, Ys[i + 1]], uin.at[q, y], b2_s.at[q, i], b2_r.at[q, i], y_peers[i])
+
+    def b1(q, i):
+        return remote(vout.at[q, As[i + 1]], vin.at[q, a], b1_s.at[q, i], b1_r.at[q, i], a_peers[i])
+
+    def load_up(q):
+        slot = q % 2
+        depth = pl.ds(pl.multiple_of(q * CW, CW), CW)
+        return (
+            pltpu.make_async_copy(wg_ref.at[:, depth], wgu.at[slot, :, :, 0:384], wg_m.at[slot]),
+            pltpu.make_async_copy(wu_ref.at[:, depth], wgu.at[slot, :, :, 384:768], wu_m.at[slot]),
+        )
+
+    def load_down(q):
+        return pltpu.make_async_copy(
+            wd_ref.at[:, :, q * CW : (q + 1) * CW], wdn.at[q % 3], wd_m.at[q]
+        )
+
+    lane = lax.broadcasted_iota(jnp.int32, (32, 128), 1)
+    named = jnp.zeros((32, 128), F32)
+    gate = jnp.zeros((32, 128), F32)
+    for k in range(8):
+        hit = routes_ref[:, k : k + 1] == lane % 64
+        named = named + jnp.where(hit, 1.0, 0.0)
+        gate = gate + jnp.where(hit, gates_ref[:, k : k + 1], 0.0)
+    before = (
+        lax.broadcasted_iota(jnp.int32, (32, 32), 1) < lax.broadcasted_iota(jnp.int32, (32, 32), 0)
+    )
+    rank = jnp.dot(
+        jnp.where(before, 1.0, 0.0).astype(BF), named.astype(BF), preferred_element_type=F32
+    )
+    meta[y, a] = jnp.where(lane < 64, jnp.where(named > 0.5, rank, -1.0), gate).astype(BF)
+    for i in range(3):
+        m1(i).start()
+
+    def first(q, carry):
+        tok[q, y, a] = normed_ref[q]
+        for i in range(3):
+            s1(q, i).start()
+        return carry
+
+    lax.fori_loop(0, CH, first, 0)
+    for q in range(2):
+        for copy in load_up(q):
+            copy.start()
+    for q in range(3):
+        load_down(q).start()
+    for i in range(3):
+        m1(i).wait()
+    for i in range(3):
+        m2(i).start()
+
+    def second(q, carry):
+        for i in range(3):
+            s1(q, i).wait()
+        for i in range(3):
+            s2(q, i).start()
+        return carry
+
+    lax.fori_loop(0, CH, second, 0)
+    for i in range(3):
+        m2(i).wait()
+
+    info = meta[...].reshape(512, 128)
+    base = a * (16 * (1 - core) + 4 * core) + 2 * yl
+    step_c = 4 * (1 - core) + 16 * core
+    m_lane = lax.broadcasted_iota(jnp.int32, (128, 128), 1)
+    l_row = lax.broadcasted_iota(jnp.int32, (128, 128), 0)
+    want = base + (m_lane // 2) * step_c + m_lane % 2
+    pick_rank = jnp.where((l_row == want) & (m_lane < 8), 1.0, 0.0).astype(BF)
+    pick_gate = jnp.where((l_row == want + 64) & (m_lane < 8), 1.0, 0.0).astype(BF)
+    rank_col = jnp.dot(info, pick_rank, preferred_element_type=F32)
+    gate_col = jnp.dot(info, pick_gate, preferred_element_type=F32)
+    m_row = lax.broadcasted_iota(jnp.int32, (16, 128), 0)
+    l_lane = lax.broadcasted_iota(jnp.int32, (16, 128), 1)
+    pick_row = jnp.where(
+        l_lane == base + (m_row // 2) * step_c + m_row % 2, 1.0, 0.0
+    ).astype(BF)
+    rank_row = lax.dot_general(
+        pick_row, info, (((1,), (1,)), ((), ())), preferred_element_type=F32
+    )
+    src_row = (lax.broadcasted_iota(jnp.int32, (16, 512), 1) // 32).astype(F32)
+    code_row = jnp.where(rank_row > -0.5, src_row * 6.0 + rank_row, -1.0)
+    src_col = (lax.broadcasted_iota(jnp.int32, (512, 128), 0) // 32).astype(F32)
+    code_col = jnp.where(rank_col > -0.5, src_col * 6.0 + rank_col, -1000.0)
+    at_row = lax.broadcasted_iota(jnp.int32, (96, 512), 0).astype(F32)
+    at_col = lax.broadcasted_iota(jnp.int32, (512, 768), 1).astype(F32)
+    weight = jnp.zeros((512, 768), F32)
+    for m in range(8):
+        pick[m // 2, (m % 2) * 96 : (m % 2 + 1) * 96] = jnp.where(
+            at_row == code_row[m : m + 1], 1.0, 0.0
+        ).astype(BF)
+        weight = weight + jnp.where(
+            at_col == code_col[:, m : m + 1] + (96.0 * m), gate_col[:, m : m + 1], 0.0
+        )
+    give[...] = weight.astype(BF)
+
+    def select(q):
+        for i in range(3):
+            s2(q, i).wait_recv()
+
+        def one(o):
+            p = pick[lax.rem(c + o, 4)]
+            parts = [
+                jnp.dot(
+                    p,
+                    tok[q, :, :, :, n * 256 : (n + 1) * 256].reshape(512, 256),
+                    preferred_element_type=F32,
+                ).astype(BF).reshape(2, 96, 256)
+                for n in range(CW // 256)
+            ]
+            return parts
+
+        def other(i, carry):
+            for n, part in enumerate(one(i + 1)):
+                stage[q, i, :, :, n * 256 : (n + 1) * 256] = part
+            return carry
+
+        lax.fori_loop(0, 3, other, 0)
+        for i in range(3):
+            s3(q, i).start()
+        for n, part in enumerate(one(0)):
+            rows[q, 0, :, c, :, n * 256 : (n + 1) * 256] = part
+
+    def share(q):
+        for i in range(3):
+            s3(q, i).wait_recv()
+        s4(q).start()
+
+    def up(q):
+        for copy in load_up(q):
+            copy.wait()
+        s4(q).wait_recv()
+        slot = q % 2
+
+        def one(i, carry):
+            s, j = i // 2, i % 2
+            r = rows[q, s, j].reshape(384, CW)
+            for n in range(3):
+                cols = slice(n * 256, (n + 1) * 256)
+                d = jnp.dot(r, wgu[slot, j, :, cols], preferred_element_type=F32)
+                acc[s, j, :, cols] = acc[s, j, :, cols] + d
+            return carry
+
+        lax.fori_loop(0, 4, one, 0)
+
+        @pl.when(q < CH - 2)
+        def _():
+            for copy in load_up(q + 2):
+                copy.start()
+
+    acc[...] = jnp.zeros_like(acc)
+
+    def dispatch(step, carry):
+        @pl.when(step < CH)
+        def _():
+            select(step)
+
+        @pl.when((step >= 1) & (step < CH + 1))
+        def _():
+            share(step - 1)
+
+        @pl.when(step >= 2)
+        def _():
+            up(step - 2)
+
+        return carry
+
+    lax.fori_loop(0, CH + 2, dispatch, 0)
+
+    def activate(i, carry):
+        s, j = i // 2, i % 2
+        v = acc[s, j, :, 0:384]
+        hid[s, j] = (v / (1.0 + jnp.exp(-v)) * acc[s, j, :, 384:768]).astype(BF)
+        return carry
+
+    lax.fori_loop(0, 4, activate, 0)
+    for q in range(3):
+        load_down(q).wait()
+
+    def down(q, s, j, n):
+        return jnp.dot(
+            hid[s, j], wdn[lax.rem(q, 3), j, :, n * 256 : (n + 1) * 256], preferred_element_type=F32
+        )
+
+    def half(step, carry):
+        @pl.when(step < CH)
+        def _():
+            def one(j, carry):
+                for n in range(CW // 256):
+                    rows[step, 1, j, :, :, n * 256 : (n + 1) * 256] = (
+                        down(step, 1, j, n).astype(BF).reshape(4, 96, 256)
+                    )
+                return carry
+
+            lax.fori_loop(0, 2, one, 0)
+            yb(step).start()
+
+        @pl.when(step >= 1)
+        def _():
+            q = step - 1
+            s4(q).wait_send()
+            yb(q).wait_recv()
+
+            def one(j, carry):
+                for n in range(CW // 256):
+                    cols = slice(n * 256, (n + 1) * 256)
+                    v = down(q, 0, j, n).reshape(4, 96, 256) + back[q, j, :, :, cols].astype(F32)
+                    rows[q, 0, j, :, :, cols] = v.astype(BF)
+                return carry
+
+            lax.fori_loop(0, 2, one, 0)
+            for i in range(3):
+                b3(q, i).start()
+            zin[q, c] = rows[q, 0, :, c]
+
+            @pl.when(q == 0)
+            def _():
+                load_down(3).start()
+
+            @pl.when(q == 1)
+            def _():
+                load_down(3).wait()
+
+        return carry
+
+    lax.fori_loop(0, CH + 1, half, 0)
+
+    def combine(step, carry):
+        @pl.when(step < CH)
+        def _():
+            q = step
+            for i in range(3):
+                b3(q, i).wait_recv()
+            for i in range(3):
+                s2(q, i).wait_send()
+
+            def one(y_):
+                g = give[pl.ds(pl.multiple_of(y_ * 128, 128), 128)]
+                return [
+                    jnp.dot(
+                        g,
+                        zin[q, :, :, :, n * 256 : (n + 1) * 256].reshape(768, 256),
+                        preferred_element_type=F32,
+                    ).astype(BF).reshape(4, 32, 256)
+                    for n in range(CW // 256)
+                ]
+
+            def other(i, carry):
+                y_ = lax.rem(y + i + 1, 4)
+                for n, part in enumerate(one(y_)):
+                    tok[q, y_, :, :, n * 256 : (n + 1) * 256] = part
+                return carry
+
+            lax.fori_loop(0, 3, other, 0)
+            for i in range(3):
+                b2(q, i).start()
+            for n, part in enumerate(one(y)):
+                uin[q, y, :, :, n * 256 : (n + 1) * 256] = part
+
+        @pl.when((step >= 1) & (step < CH + 1))
+        def _():
+            q = step - 1
+            for i in range(3):
+                b2(q, i).wait_recv()
+            v = uin[q, 0].astype(F32) + uin[q, 1].astype(F32)
+            v = v + uin[q, 2].astype(F32) + uin[q, 3].astype(F32)
+            vout[q] = v.astype(BF)
+            for i in range(3):
+                b1(q, i).start()
+            vin[q, a] = vout[q, a]
+
+        @pl.when(step >= 2)
+        def _():
+            q = step - 2
+            for i in range(3):
+                b1(q, i).wait_recv()
+            v = vin[q, 0].astype(F32) + vin[q, 1].astype(F32)
+            v = v + vin[q, 2].astype(F32) + vin[q, 3].astype(F32)
+            out_ref[:, pl.ds(pl.multiple_of(q * CW, CW), CW)] = (hsum_ref[q] + v).astype(BF)
+
+        return carry
+
+    lax.fori_loop(0, CH + 2, combine, 0)
+
+    def finish(q, carry):
+        yb(q).wait_send()
+        for i in range(3):
+            s3(q, i).wait_send()
+            b3(q, i).wait_send()
+            b2(q, i).wait_send()
+            b1(q, i).wait_send()
+        return carry
+
+    lax.fori_loop(0, CH, finish, 0)
+
+
+def mixture(normed, hsum, routes, gates, w_gate, w_up, w_down):
+    dma = pltpu.SemaphoreType.DMA
+    vm = pl.BlockSpec(memory_space=pltpu.VMEM)
+    hbm = pl.BlockSpec(memory_space=pl.ANY)
+    return pl.pallas_call(
+        experts_kernel,
+        out_shape=jax.ShapeDtypeStruct((32, D), BF),
+        in_specs=[vm] * 4 + [hbm] * 3,
+        out_specs=vm,
+        scratch_shapes=[
+            pltpu.VMEM((CH, 4, 4, 32, CW), BF),
+            pltpu.VMEM((4, 4, 32, 128), BF),
+            pltpu.VMEM((CH, 3, 2, 96, CW), BF),
+            pltpu.VMEM((CH, 2, 2, 4, 96, CW), BF),
+            pltpu.VMEM((2, 2, 384, 768), F32),
+            pltpu.VMEM((2, 2, 384, 384), BF),
+            pltpu.VMEM((2, 2, CW, 768), BF),
+            pltpu.VMEM((3, 2, 384, CW), BF),
+            pltpu.VMEM((CH, 2, 4, 96, CW), BF),
+            pltpu.VMEM((CH, 4, 2, 96, CW), BF),
+            pltpu.VMEM((CH, 4, 4, 32, CW), BF),
+            pltpu.VMEM((CH, 4, 32, CW), BF),
+            pltpu.VMEM((CH, 4, 32, CW), BF),
+            pltpu.VMEM((4, 192, 512), BF),
+            pltpu.VMEM((512, 768), BF),
+            dma((6,)), dma((6,)),
+            dma((CH, 3)), dma((CH, 3)), dma((CH, 3)), dma((CH, 3)), dma((CH, 3)), dma((CH, 3)),
+            dma((CH,)), dma((CH,)), dma((CH,)), dma((CH,)),
+            dma((CH, 3)), dma((CH, 3)), dma((CH, 3)), dma((CH, 3)), dma((CH, 3)), dma((CH, 3)),
+            dma((2,)), dma((2,)), dma((CH,)),
+        ],
+        compiler_params=pltpu.CompilerParams(
+            collective_id=1, has_side_effects=True, vmem_limit_bytes=63 * 2**20
+        ),
+        cost_estimate=pl.CostEstimate(
+            flops=20 * 10**9, bytes_accessed=20 * 2**20, transcendentals=2**20
+        ),
+    )(normed, hsum, routes, gates, w_gate, w_up, w_down)
 
 
 def shards(
     queries, keys, values, resid, out_weight, norm_gain, routes, gates, w_gate, w_up, w_down
 ):
-    n_ctx = lax.axis_size("context")
     hsum, normed = attention(queries, keys, values, out_weight, resid, norm_gain)
-    hsum = hsum.transpose(1, 0, 2).reshape(32, D)
-    normed = normed.transpose(1, 0, 2).reshape(32, D)
-    tok_own = resid.shape[0]
-    topk = routes.shape[1]
-    experts = EXP_DEV * n_ctx
-    capacity = max(2, 3 * tok_own * topk // (2 * experts))
-    flat = routes.reshape(-1)
-    onehot = (flat[:, None] == jnp.arange(experts, dtype=jnp.int32)[None, :]).astype(jnp.int32)
-    slots = jnp.sum((jnp.cumsum(onehot, axis=0) - onehot) * onehot, axis=1)
-    place = flat * capacity + slots
-    outgoing = (
-        jnp.zeros((experts * capacity, D), jnp.bfloat16)
-        .at[place]
-        .set(jnp.repeat(normed, topk, axis=0))
-    )
-    outgoing = outgoing.reshape(n_ctx, EXP_DEV, capacity, D)
-    arrived = lax.all_to_all(outgoing, "context", split_axis=0, concat_axis=0, tiled=True)
-    shared = lax.all_gather(arrived, "tensor", axis=0, tiled=True)
-    gating = jnp.einsum("sjcd,jdf->sjcf", shared, w_gate, preferred_element_type=jnp.float32)
-    upward = jnp.einsum("sjcd,jdf->sjcf", shared, w_up, preferred_element_type=jnp.float32)
-    hidden = (jax.nn.silu(gating) * upward).astype(jnp.bfloat16)
-    reduced = lax.psum_scatter(
-        jnp.einsum("sjcf,jfd->sjcd", hidden, w_down, preferred_element_type=jnp.float32).astype(
-            jnp.bfloat16
-        ),
-        "tensor",
-        scatter_dimension=0,
-        tiled=True,
-    )
-    results = lax.all_to_all(reduced, "context", split_axis=0, concat_axis=0, tiled=True)
-    picked = results.reshape(experts * capacity, D)[place]
-    contrib = jnp.einsum("tk,tkd->td", gates, picked.reshape(tok_own, topk, D).astype(jnp.float32))
-    return (hsum + contrib).astype(jnp.bfloat16)
+    return mixture(normed, hsum, routes, gates, w_gate, w_up, w_down)
 
 
 def solution(mesh):

time: 483 us -> 267 us (0.55)
  waiting for transfers between devices: 230 us -> 0 us
  Pallas kernels: 97.1 us -> 262 us
  blocking collectives: 58.7 us -> 0 us
  local copies, waits for them, and re-layouts: 39.3 us -> 4.39 us
  matrix products: 33.3 us -> 0 us
  between operations: 13.5 us -> 0.02 us
  starting transfers between devices: 7.65 us -> 0 us
    pallas_call x0 -> x1, Pallas kernels: none -> 165 us  [mixture(): pl.pallas_call(experts_kernel, out_shape=jax.ShapeDtypeStruct((32, D), BF...]
    reduce_scatter x1 -> x0, waiting for transfers between devices: 106 us -> none  [shards(): lax.psum_scatter(jnp.einsum('sjcf,jfd->sjcd', hidden, w_down, preferred_e...]
    all_gather x1 -> x0, waiting for transfers between devices: 83.9 us -> none  [shards(): shared = lax.all_gather(arrived, 'tensor', axis=0, tiled=True)]
    all_to_all x1 -> x0, blocking collectives: 58.7 us -> none  [shards(): lax.all_to_all(outgoing, 'context', split_axis=0, concat_axis=0, tiled=True)]
    all_to_all x1 -> x0, waiting for transfers between devices: 40.1 us -> none  [shards(): lax.all_to_all(reduced, 'context', split_axis=0, concat_axis=0, tiled=True)]
    dot_general x4 -> x0, matrix products: 33.3 us -> none  [the longest x1 12.3 us: shards(): jnp.einsum('sjcd,jdf->sjcf', shared, w_up, preferred_element_type=jnp.flo...]
    reshape x5 -> x0, local copies, waits for them, and re-layouts: 15.4 us -> none  [the longest x2 8.34 us: shards(): outgoing = outgoing.reshape(n_ctx, EXP_DEV, capacity, D)]
    all_to_all x2 -> x0, local copies, waits for them, and re-layouts: 8.06 us -> none  [the longest x1 4.28 us: shards(): lax.all_to_all(reduced, 'context', split_axis=0, concat_axis=0, tiled=True)]
  transfers between devices with their start and end apart: 3 -> 0, of which waited for: 3 -> 0; matrix products, arithmetic and copies ran while one was open for 0% -> 0% of each run, Pallas kernels for 0% -> 0%
where the time goes in v2:
time: 267 us
  Pallas kernels  262 us (98%)
  local copies, waits for them, and re-layouts  4.39 us (2%)
    pallas_call x1, Pallas kernels, mixture(): pl.pallas_call(experts_kernel, out_shape=jax.ShapeDtypeStruct((32, D), BF...  165 us
    pallas_call x1, Pallas kernels, attention(): pl.pallas_call(attention_kernel, out_shape=(jax.ShapeDtypeStruct((4, 32,...  97 us

profile of v2, /device:TPU:0, one launch (start us, length us, event | category | flops | bytes accessed | tf_op | source)
XLA Modules:
  0.0 266.8 jit_solution(6728094848209299179)
XLA Ops:
  0.0 1.4 copy.12.routes_ref
  1.4 1.4 copy.13.gates_ref
  2.7 97.0 %shard_map.109 = (f32[4,32,1024]{2,1,0:T(8,128)}, bf16[4,32,1024]{2,1,0:T(8,128)(2,1)}) custom-call(bf16[128,2048]{1,0:T(8,128)(2,1)} %q_ref.1, bf16[128,128]{1,0:T(8,128)(2,1)} %k_ref.1, bf16[128,128]{1,0:T(8,128)(2,1)} %v_ref.1, bf16[2048,128]{1,0:T(8,128)(2,1)} %w_ref.1, bf16[32,4096]{1,0:T(8,128)(2,1)} %resid_ref.1, f32[1,4096]{1,0:T(1,128)} %bitcast.1), custom_call_target="tpu_custom_call" | custom-call | flops 8000000000 | bytes 4194304 | tf_op jit(solution)/shard_map/pallas_call | solution.py:195
  99.8 165.3 %shard_map.110 = bf16[32,4096]{1,0:T(8,128)(2,1)} custom-call(bf16[4,32,1024]{2,1,0:T(8,128)(2,1)} %get-tuple-element.7.normed_ref, f32[4,32,1024]{2,1,0:T(8,128)} %get-tuple-element.8.hsum_ref, s32[32,8]{1,0:T(8,128)} %copy.12.routes_ref, f32[32,8]{1,0:T(8,128)} %copy.13.gates_ref, bf16[2,4096,384]{2,1,0:T(8,128)(2,1)} %wg_ref.1, ...), custom_call_target="tpu_custom_call" | custom-call | flops 20000000000 | bytes 20971520 | tf_op jit(solution)/shard_map/pallas_call | solution.py:588
  265.1 1.7 copy.15

commit v3 on v2

--- a/solution.py
+++ b/solution.py
@@ -52,36 +52,79 @@
     z_peers = [device(zs[o], x, yl, yh, core) for o in (1, 2, 3)]
     x_peers = [device(z, xs[o], yl, yh, core) for o in (1, 2, 3)]
     y_peer = device(z, x, 1 - yl, yh, core)
-    w_peers = [device(z, xs[o], lax.rem(yl + p, 2), yh, core) for o, p in group]
     o_peers = [device(zs[o], x, yl, lax.rem(yh + p, 2), core) for o, p in group]
-    greet([sibling] + z_peers + w_peers + [device(zs[o], x, yl, 1 - yh, core) for o in range(4)])
+    greet([sibling, y_peer] + z_peers + x_peers + [device(zs[o], x, yl, 1 - yh, core) for o in range(4)])
 
     kall[z, x, yl] = k_ref[...]
     vall[z, x, yl] = v_ref[...]
     me = (z, x, yl)
+    mine = pl.ds(pl.multiple_of((x * 2 + yl) * 128, 128), 128)
+    both = pl.ds(pl.multiple_of(x * 256, 256), 256)
+    low, high = pl.ds(0, 1024), pl.ds(1024, 1024)
+    wall[:, mine] = w_ref[...]
+
+    def wa1():
+        return [send(w_ref.at[low], wall.at[low, mine], w_s.at[0], w_r.at[0], y_peer)]
+
+    def wb1():
+        return [
+            send(w_ref.at[high], wall.at[high, mine], w_s.at[1 + i], w_r.at[1 + i], x_peers[i])
+            for i in range(3)
+        ]
+
     k1 = [send(kall.at[me], kall.at[me], k_s.at[i], k_r.at[i], z_peers[i]) for i in range(3)]
     v1 = [send(vall.at[me], vall.at[me], v_s.at[0], v_r.at[0], y_peer)]
-    for copy in v1 + k1:
+    for copy in v1:
+        copy.wait_recv()
+    v2 = [
+        send(vall.at[z, x], vall.at[z, x], v_s.at[1 + i], v_r.at[1 + i], x_peers[i])
+        for i in range(3)
+    ]
+    v3 = []
+    k3 = []
+
+    def v_on(p, x_):
+        for i in range(3):
+            n = 4 + 3 * p + i
+            v3.append(send(vall.at[z, x_], vall.at[z, x_], v_s.at[n], v_r.at[n], z_peers[i]))
+
+    def k_on(p, x_):
+        n = 6 + p
+        k3.append(send(kall.at[:, x_, yl], kall.at[:, x_, yl], k_s.at[n], k_r.at[n], y_peer))
+
+    v_on(0, x)
+    for copy in k1:
         copy.wait_recv()
     k2 = [
         send(kall.at[:, x, yl], kall.at[:, x, yl], k_s.at[3 + i], k_r.at[3 + i], x_peers[i])
         for i in range(3)
     ]
-    v2 = [
-        send(vall.at[z, x], vall.at[z, x], v_s.at[1 + i], v_r.at[1 + i], x_peers[i])
+    k_on(0, x)
+    for i in range(3):
+        x_ = lax.rem(x + 3 - i, 4)
+        v2[i].wait_recv()
+        v_on(1 + i, x_)
+        k2[i].wait_recv()
+        k_on(1 + i, x_)
+    w1 = wb1() + wa1()
+    w1[3].wait_recv()
+    w2 = [
+        send(wall.at[low, both], wall.at[low, both], w_s.at[4 + i], w_r.at[4 + i], x_peers[i])
         for i in range(3)
     ]
-    for copy in v2 + k2:
-        copy.wait_recv()
-    k3 = [send(kall.at[:, :, yl], kall.at[:, :, yl], k_s.at[6], k_r.at[6], y_peer)]
-    v3 = [send(vall.at[z], vall.at[z], v_s.at[4 + i], v_r.at[4 + i], z_peers[i]) for i in range(3)]
-    mine = pl.ds(pl.multiple_of((x * 2 + yl) * 128, 128), 128)
-    wcopies = [
-        send(w_ref, wall.at[:, mine], w_s.at[i], w_r.at[i], w_peers[i]) for i in range(7)
-    ]
-    wall[:, mine] = w_ref[...]
+
+    def wb2(p, x_):
+        cols = pl.ds(pl.multiple_of((x_ * 2 + yl) * 128, 128), 128)
+        w2.append(send(wall.at[high, cols], wall.at[high, cols], w_s.at[7 + p], w_r.at[7 + p], y_peer))
+
+    wb2(0, x)
     for copy in v3 + k3:
         copy.wait_recv()
+
+    def forward():
+        for i in range(3):
+            w1[i].wait_recv()
+            wb2(1 + i, lax.rem(x + 3 - i, 4))
 
     factor = HW**-0.5 * 1.4426950408889634
     last = ctx // 4
@@ -140,8 +183,10 @@
             send(att.at[z, hc], att.at[z, hc], a_s.at[hc, i], a_r.at[hc, i], z_peers[i])
         return carry
 
-    lax.fori_loop(0, 4, heads, 0)
-    for copy in wcopies:
+    lax.fori_loop(0, 1, heads, 0)
+    forward()
+    lax.fori_loop(1, 4, heads, 0)
+    for copy in w2:
         copy.wait_recv()
 
     def project(hc, carry):
@@ -185,7 +230,7 @@
     scale = lax.rsqrt(square * (1.0 / D) + 1e-06)
     for n in range(4):
         normed_ref[n] = (hsum_ref[n] * scale * gain_ref[:, n * 1024 : (n + 1) * 1024]).astype(BF)
-    for copy in k1 + k2 + k3 + v1 + v2 + v3 + wcopies:
+    for copy in k1 + k2 + k3 + v1 + v2 + v3 + w1 + w2:
         copy.wait_send()
 
 
@@ -211,7 +256,7 @@
             pltpu.VMEM((4, 2, 32, 1024), BF),
             pltpu.VMEM((4, 2, 32, 1024), BF),
             pltpu.VMEM((4, 2, 32, 1024), BF),
-            dma((7,)), dma((7,)), dma((7,)), dma((7,)), dma((7,)), dma((7,)),
+            dma((10,)), dma((10,)), dma((16,)), dma((16,)), dma((11,)), dma((11,)),
             dma((4, 3)), dma((4, 3)), dma((1,)), dma((1,)), dma((7,)), dma((7,)),
         ],
         compiler_params=pltpu.CompilerParams(
@@ -223,11 +268,13 @@
 
 CH = 4
 CW = D // CH
+AHEAD = 2
+BACK = 2
 
 
 def experts_kernel(
     normed_ref, hsum_ref, routes_ref, gates_ref, wg_ref, wu_ref, wd_ref, out_ref,
-    tok, meta, stage, rows, acc, hid, wgu, wdn, back, zin, uin, vout, vin, pick, give,
+    tok, meta, stage, rows, acc, hid, wgu, wdn, back, zin, uin, uhalf, vout, vin, pick, give,
     m_s, m_r, s1_s, s1_r, s2_s, s2_r, s3_s, s3_r, s4_s, s4_r,
     y_s, y_r, b3_s, b3_r, b2_s, b2_r, b1_s, b1_r, wg_m, wu_m, wd_m,
 ):
@@ -264,8 +311,16 @@
     def s1(q, i):
         return remote(normed_ref.at[q], tok.at[q, y, a], s1_s.at[q, i], s1_r.at[q, i], a_peers[i])
 
+    ends = (y_peers[0], y_peers[2])
+    Yn = (Ys[1], Ys[3])
+    parts = (pl.ds(0, 2), pl.ds(2, 2))
+
     def s2(q, i):
-        return remote(tok.at[q, y], tok.at[q, y], s2_s.at[q, i], s2_r.at[q, i], y_peers[i])
+        return remote(tok.at[q, y], tok.at[q, y], s2_s.at[q, i], s2_r.at[q, i], ends[i])
+
+    def relay(q, i):
+        block = tok.at[q, Yn[1 - i], parts[i]]
+        return remote(block, block, s2_s.at[q, 2 + i], s2_r.at[q, 2 + i], ends[i])
 
     def s3(q, i):
         return remote(
@@ -284,7 +339,11 @@
         )
 
     def b2(q, i):
-        return remote(tok.at[q, Ys[i + 1]], uin.at[q, y], b2_s.at[q, i], b2_r.at[q, i], y_peers[i])
+        return remote(tok.at[q, Yn[i]], uin.at[q, i], b2_s.at[q, i], b2_r.at[q, i], ends[i])
+
+    def far(q, i):
+        block = tok.at[q, Ys[2], parts[i]]
+        return remote(block, uhalf.at[q, i], b2_s.at[q, 2 + i], b2_r.at[q, 2 + i], ends[i])
 
     def b1(q, i):
         return remote(vout.at[q, As[i + 1]], vin.at[q, a], b1_s.at[q, i], b1_r.at[q, i], a_peers[i])
@@ -298,9 +357,8 @@
         )
 
     def load_down(q):
-        return pltpu.make_async_copy(
-            wd_ref.at[:, :, q * CW : (q + 1) * CW], wdn.at[q % 3], wd_m.at[q]
-        )
+        cols = pl.ds(pl.multiple_of(q * CW, CW), CW)
+        return pltpu.make_async_copy(wd_ref.at[:, :, cols], wdn.at[q % 3], wd_m.at[q % 3])
 
     lane = lax.broadcasted_iota(jnp.int32, (32, 128), 1)
     named = jnp.zeros((32, 128), F32)
@@ -336,14 +394,14 @@
     for i in range(3):
         m2(i).start()
 
-    def second(q, carry):
+    def second(q):
         for i in range(3):
             s1(q, i).wait()
-        for i in range(3):
+        for i in range(2):
             s2(q, i).start()
-        return carry
-
-    lax.fori_loop(0, CH, second, 0)
+
+    for q in range(AHEAD):
+        second(q)
     for i in range(3):
         m2(i).wait()
 
@@ -381,9 +439,19 @@
         )
     give[...] = weight.astype(BF)
 
+    def pass_on(q):
+        for i in range(2):
+            s2(q, i).wait_recv()
+        for i in range(2):
+            relay(q, i).start()
+
+        @pl.when(q + AHEAD < CH)
+        def _():
+            second(q + AHEAD)
+
     def select(q):
-        for i in range(3):
-            s2(q, i).wait_recv()
+        for i in range(2):
+            relay(q, i).wait_recv()
 
         def one(o):
             p = pick[lax.rem(c + o, 4)]
@@ -440,19 +508,23 @@
     def dispatch(step, carry):
         @pl.when(step < CH)
         def _():
-            select(step)
+            pass_on(step)
 
         @pl.when((step >= 1) & (step < CH + 1))
         def _():
-            share(step - 1)
-
-        @pl.when(step >= 2)
-        def _():
-            up(step - 2)
+            select(step - 1)
+
+        @pl.when((step >= 2) & (step < CH + 2))
+        def _():
+            share(step - 2)
+
+        @pl.when(step >= 3)
+        def _():
+            up(step - 3)
 
         return carry
 
-    lax.fori_loop(0, CH + 2, dispatch, 0)
+    lax.fori_loop(0, CH + 3, dispatch, 0)
 
     def activate(i, carry):
         s, j = i // 2, i % 2
@@ -461,8 +533,6 @@
         return carry
 
     lax.fori_loop(0, 4, activate, 0)
-    for q in range(3):
-        load_down(q).wait()
 
     def down(q, s, j, n):
         return jnp.dot(
@@ -472,6 +542,8 @@
     def half(step, carry):
         @pl.when(step < CH)
         def _():
+            load_down(step).wait()
+
             def one(j, carry):
                 for n in range(CW // 256):
                     rows[step, 1, j, :, :, n * 256 : (n + 1) * 256] = (
@@ -496,86 +568,101 @@
                 return carry
 
             lax.fori_loop(0, 2, one, 0)
+            @pl.when(q < BACK)
+            def _():
+                for i in range(3):
+                    b3(q, i).start()
+
+            zin[q, c] = rows[q, 0, :, c]
+
+            @pl.when(q < CH - 3)
+            def _():
+                load_down(q + 3).start()
+
+        return carry
+
+    lax.fori_loop(0, CH + 1, half, 0)
+
+    def one_sum(q, o):
+        y_ = Ys[o]
+        g = give[pl.ds(pl.multiple_of(y_ * 128, 128), 128)]
+        for n in range(CW // 256):
+            cols = slice(n * 256, (n + 1) * 256)
+            tok[q, y_, :, :, cols] = jnp.dot(
+                g, zin[q, :, :, :, cols].reshape(768, 256), preferred_element_type=F32
+            ).astype(BF).reshape(4, 32, 256)
+
+    def gather_sums(q):
+        for i in range(3):
+            b3(q, i).wait_recv()
+
+        @pl.when(q + BACK < CH)
+        def _():
             for i in range(3):
-                b3(q, i).start()
-            zin[q, c] = rows[q, 0, :, c]
-
-            @pl.when(q == 0)
-            def _():
-                load_down(3).start()
-
-            @pl.when(q == 1)
-            def _():
-                load_down(3).wait()
+                b3(q + BACK, i).start()
+
+        for i in range(2):
+            s2(q, i).wait_send()
+            relay(q, i).wait_send()
+        one_sum(q, 2)
+        for i in range(2):
+            far(q, i).start()
+        for o in (1, 3, 0):
+            one_sum(q, o)
+
+    def add_half(q):
+        for i in range(2):
+            far(q, i).wait_recv()
+            block = tok[q, Yn[i], parts[i]].astype(F32) + uhalf[q, i].astype(F32)
+            tok[q, Yn[i], parts[i]] = block.astype(BF)
+            b2(q, i).start()
+
+    def along(q):
+        for i in range(2):
+            b2(q, i).wait_recv()
+        v = uin[q, 0].astype(F32) + uin[q, 1].astype(F32) + tok[q, y].astype(F32)
+        vout[q] = v.astype(BF)
+        for i in range(3):
+            b1(q, i).start()
+        vin[q, a] = vout[q, a]
+
+    def store(q):
+        for i in range(3):
+            b1(q, i).wait_recv()
+        v = vin[q, 0].astype(F32) + vin[q, 1].astype(F32)
+        v = v + vin[q, 2].astype(F32) + vin[q, 3].astype(F32)
+        out_ref[:, pl.ds(pl.multiple_of(q * CW, CW), CW)] = (hsum_ref[q] + v).astype(BF)
+
+    def combine(step, carry):
+        @pl.when((step >= 1) & (step < CH + 1))
+        def _():
+            add_half(step - 1)
+
+        @pl.when(step < CH)
+        def _():
+            gather_sums(step)
+
+        @pl.when((step >= 2) & (step < CH + 2))
+        def _():
+            along(step - 2)
+
+        @pl.when(step >= 3)
+        def _():
+            store(step - 3)
 
         return carry
 
-    lax.fori_loop(0, CH + 1, half, 0)
-
-    def combine(step, carry):
-        @pl.when(step < CH)
-        def _():
-            q = step
-            for i in range(3):
-                b3(q, i).wait_recv()
-            for i in range(3):
-                s2(q, i).wait_send()
-
-            def one(y_):
-                g = give[pl.ds(pl.multiple_of(y_ * 128, 128), 128)]
-                return [
-                    jnp.dot(
-                        g,
-                        zin[q, :, :, :, n * 256 : (n + 1) * 256].reshape(768, 256),
-                        preferred_element_type=F32,
-                    ).astype(BF).reshape(4, 32, 256)
-                    for n in range(CW // 256)
-                ]
-
-            def other(i, carry):
-                y_ = lax.rem(y + i + 1, 4)
-                for n, part in enumerate(one(y_)):
-                    tok[q, y_, :, :, n * 256 : (n + 1) * 256] = part
-                return carry
-
-            lax.fori_loop(0, 3, other, 0)
-            for i in range(3):
-                b2(q, i).start()
-            for n, part in enumerate(one(y)):
-                uin[q, y, :, :, n * 256 : (n + 1) * 256] = part
-
-        @pl.when((step >= 1) & (step < CH + 1))
-        def _():
-            q = step - 1
-            for i in range(3):
-                b2(q, i).wait_recv()
-            v = uin[q, 0].astype(F32) + uin[q, 1].astype(F32)
-            v = v + uin[q, 2].astype(F32) + uin[q, 3].astype(F32)
-            vout[q] = v.astype(BF)
-            for i in range(3):
-                b1(q, i).start()
-            vin[q, a] = vout[q, a]
-
-        @pl.when(step >= 2)
-        def _():
-            q = step - 2
-            for i in range(3):
-                b1(q, i).wait_recv()
-            v = vin[q, 0].astype(F32) + vin[q, 1].astype(F32)
-            v = v + vin[q, 2].astype(F32) + vin[q, 3].astype(F32)
-            out_ref[:, pl.ds(pl.multiple_of(q * CW, CW), CW)] = (hsum_ref[q] + v).astype(BF)
-
-        return carry
-
-    lax.fori_loop(0, CH + 2, combine, 0)
+    lax.fori_loop(0, CH + 3, combine, 0)
 
     def finish(q, carry):
         yb(q).wait_send()
         for i in range(3):
             s3(q, i).wait_send()
             b3(q, i).wait_send()
+            b1(q, i).wait_send()
+        for i in range(2):
+            far(q, i).wait_send()
             b2(q, i).wait_send()
-            b1(q, i).wait_send()
         return carry
 
     lax.fori_loop(0, CH, finish, 0)
@@ -601,16 +688,17 @@
             pltpu.VMEM((3, 2, 384, CW), BF),
             pltpu.VMEM((CH, 2, 4, 96, CW), BF),
             pltpu.VMEM((CH, 4, 2, 96, CW), BF),
-            pltpu.VMEM((CH, 4, 4, 32, CW), BF),
+            pltpu.VMEM((CH, 2, 4, 32, CW), BF),
+            pltpu.VMEM((CH, 2, 2, 32, CW), BF),
             pltpu.VMEM((CH, 4, 32, CW), BF),
             pltpu.VMEM((CH, 4, 32, CW), BF),
             pltpu.VMEM((4, 192, 512), BF),
             pltpu.VMEM((512, 768), BF),
             dma((6,)), dma((6,)),
-            dma((CH, 3)), dma((CH, 3)), dma((CH, 3)), dma((CH, 3)), dma((CH, 3)), dma((CH, 3)),
+            dma((CH, 3)), dma((CH, 3)), dma((CH, 4)), dma((CH, 4)), dma((CH, 3)), dma((CH, 3)),
             dma((CH,)), dma((CH,)), dma((CH,)), dma((CH,)),
-            dma((CH, 3)), dma((CH, 3)), dma((CH, 3)), dma((CH, 3)), dma((CH, 3)), dma((CH, 3)),
-            dma((2,)), dma((2,)), dma((CH,)),
+            dma((CH, 3)), dma((CH, 3)), dma((CH, 4)), dma((CH, 4)), dma((CH, 3)), dma((CH, 3)),
+            dma((2,)), dma((2,)), dma((3,)),
         ],
         compiler_params=pltpu.CompilerParams(
             collective_id=1, has_side_effects=True, vmem_limit_bytes=63 * 2**20

time: 267 us -> 217 us (0.81)
  Pallas kernels: 262 us -> 212 us
    pallas_call x1, Pallas kernels: 165 us -> 137 us  [mixture(): pl.pallas_call(experts_kernel, out_shape=jax.ShapeDtypeStruct((32, D), BF...]
    pallas_call x1, Pallas kernels: 97 us -> 75.8 us  [attention(): pl.pallas_call(attention_kernel, out_shape=(jax.ShapeDtypeStruct((4, 32,...]
where the time goes in v3:
time: 217 us
  Pallas kernels  212 us (98%)
  local copies, waits for them, and re-layouts  4.39 us (2%)
    pallas_call x1, Pallas kernels, mixture(): pl.pallas_call(experts_kernel, out_shape=jax.ShapeDtypeStruct((32, D), BF...  137 us
    pallas_call x1, Pallas kernels, attention(): pl.pallas_call(attention_kernel, out_shape=(jax.ShapeDtypeStruct((4, 32,...  75.8 us
    unnamed x3, local copies, waits for them, and re-layouts  4.39 us

profile of v3, /device:TPU:0, one launch (start us, length us, event | category | flops | bytes accessed | tf_op | source)
XLA Modules:
  0.0 216.9 jit_solution(15015995800394400127)
XLA Ops:
  0.0 1.4 copy.12.routes_ref
  1.4 1.4 copy.13.gates_ref
  2.7 75.8 %shard_map.109 = (f32[4,32,1024]{2,1,0:T(8,128)}, bf16[4,32,1024]{2,1,0:T(8,128)(2,1)}) custom-call(bf16[128,2048]{1,0:T(8,128)(2,1)} %q_ref.1, bf16[128,128]{1,0:T(8,128)(2,1)} %k_ref.1, bf16[128,128]{1,0:T(8,128)(2,1)} %v_ref.1, bf16[2048,128]{1,0:T(8,128)(2,1)} %w_ref.1, bf16[32,4096]{1,0:T(8,128)(2,1)} %resid_ref.1, f32[1,4096]{1,0:T(1,128)} %bitcast.1), custom_call_target="tpu_custom_call" | custom-call | flops 8000000000 | bytes 4194304 | tf_op jit(solution)/shard_map/pallas_call | solution.py:240
  78.5 136.7 %shard_map.110 = bf16[32,4096]{1,0:T(8,128)(2,1)} custom-call(bf16[4,32,1024]{2,1,0:T(8,128)(2,1)} %get-tuple-element.7.normed_ref, f32[4,32,1024]{2,1,0:T(8,128)} %get-tuple-element.8.hsum_ref, s32[32,8]{1,0:T(8,128)} %copy.12.routes_ref, f32[32,8]{1,0:T(8,128)} %copy.13.gates_ref, bf16[2,4096,384]{2,1,0:T(8,128)(2,1)} %wg_ref.1, ...), custom_call_target="tpu_custom_call" | custom-call | flops 20000000000 | bytes 20971520 | tf_op jit(solution)/shard_map/pallas_call | solution.py:675
  215.2 1.7 copy.15

commit v4 on v3

--- a/solution.py
+++ b/solution.py
@@ -221,15 +221,16 @@
     for copy in ocopies:
         copy.wait()
     square = jnp.zeros((32, 1), F32)
-    for n in range(4):
-        h = resid_ref[:, n * 1024 : (n + 1) * 1024].astype(F32) + (
-            own_in[n, 0].astype(F32) + own_in[n, 1].astype(F32)
+    for n in range(8):
+        at, cols = n // 2, slice((n % 2) * 512, (n % 2 + 1) * 512)
+        h = resid_ref[:, n * 512 : (n + 1) * 512].astype(F32) + (
+            own_in[at, 0, :, cols].astype(F32) + own_in[at, 1, :, cols].astype(F32)
         )
         hsum_ref[n] = h
         square = square + jnp.sum(h * h, axis=1, keepdims=True)
     scale = lax.rsqrt(square * (1.0 / D) + 1e-06)
-    for n in range(4):
-        normed_ref[n] = (hsum_ref[n] * scale * gain_ref[:, n * 1024 : (n + 1) * 1024]).astype(BF)
+    for n in range(8):
+        normed_ref[n] = (hsum_ref[n] * scale * gain_ref[:, n * 512 : (n + 1) * 512]).astype(BF)
     for copy in k1 + k2 + k3 + v1 + v2 + v3 + w1 + w2:
         copy.wait_send()
 
@@ -240,8 +241,8 @@
     return pl.pallas_call(
         attention_kernel,
         out_shape=(
-            jax.ShapeDtypeStruct((4, 32, 1024), F32),
-            jax.ShapeDtypeStruct((4, 32, 1024), BF),
+            jax.ShapeDtypeStruct((8, 32, 512), F32),
+            jax.ShapeDtypeStruct((8, 32, 512), BF),
         ),
         in_specs=[vm] * 6,
         out_specs=(vm, vm),
@@ -266,8 +267,11 @@
     )(queries, keys, values, out_weight, resid, norm_gain.reshape(1, D))
 
 
-CH = 4
+CH = 8
 CW = D // CH
+OUT = tuple((q, 1) for q in range(8))
+HOME = ((0, 2), (2, 2), (4, 2), (6, 2))
+NO, NH = len(OUT), len(HOME)
 AHEAD = 2
 BACK = 2
 
@@ -297,6 +301,9 @@
     sibling = device(z, x, yl, yh, 1 - core)
     greet([sibling] + a_peers + y_peers + c_peers)
 
+    def un(g, groups=OUT):
+        return pl.ds(*groups[g])
+
     def remote(src, dst, ssem, rsem, to):
         return pltpu.make_async_remote_copy(
             src_ref=src, dst_ref=dst, send_sem=ssem, recv_sem=rsem, device_id=to, device_id_type=MESH
@@ -308,65 +315,101 @@
     def m2(i):
         return remote(meta.at[y], meta.at[y], m_s.at[3 + i], m_r.at[3 + i], y_peers[i])
 
-    def s1(q, i):
-        return remote(normed_ref.at[q], tok.at[q, y, a], s1_s.at[q, i], s1_r.at[q, i], a_peers[i])
+    def s1(g, i):
+        u = un(g)
+        return remote(normed_ref.at[u], tok.at[u, y, a], s1_s.at[g, i], s1_r.at[g, i], a_peers[i])
 
     ends = (y_peers[0], y_peers[2])
     Yn = (Ys[1], Ys[3])
     parts = (pl.ds(0, 2), pl.ds(2, 2))
 
-    def s2(q, i):
-        return remote(tok.at[q, y], tok.at[q, y], s2_s.at[q, i], s2_r.at[q, i], ends[i])
-
-    def relay(q, i):
-        block = tok.at[q, Yn[1 - i], parts[i]]
-        return remote(block, block, s2_s.at[q, 2 + i], s2_r.at[q, 2 + i], ends[i])
-
-    def s3(q, i):
+    def s2(g, i):
+        block = tok.at[un(g), y]
+        return remote(block, block, s2_s.at[g, i], s2_r.at[g, i], ends[i])
+
+    def relay(g, i):
+        block = tok.at[un(g), Yn[1 - i], parts[i]]
+        return remote(block, block, s2_s.at[g, 2 + i], s2_r.at[g, 2 + i], ends[i])
+
+    def s3(g, i):
+        u = un(g)
         return remote(
-            stage.at[q, i], rows.at[q, 0, :, c], s3_s.at[q, i], s3_r.at[q, i], c_peers[i]
-        )
-
-    def s4(q):
-        return remote(rows.at[q, 0], rows.at[q, 1], s4_s.at[q], s4_r.at[q], sibling)
-
-    def yb(q):
-        return remote(rows.at[q, 1], back.at[q], y_s.at[q], y_r.at[q], sibling)
-
-    def b3(q, i):
+            stage.at[u, i], rows.at[u, 0, :, c], s3_s.at[g, i], s3_r.at[g, i], c_peers[i]
+        )
+
+    def s4(g):
+        u = un(g)
+        return remote(rows.at[u, 0], rows.at[u, 1], s4_s.at[g], s4_r.at[g], sibling)
+
+    def yb(g):
+        u = un(g, HOME)
+        return remote(rows.at[u, 1], back.at[u], y_s.at[g], y_r.at[g], sibling)
+
+    def b3(g, i):
+        u = un(g, HOME)
         return remote(
-            rows.at[q, 0, :, Cs[i + 1]], zin.at[q, c], b3_s.at[q, i], b3_r.at[q, i], c_peers[i]
-        )
-
-    def b2(q, i):
-        return remote(tok.at[q, Yn[i]], uin.at[q, i], b2_s.at[q, i], b2_r.at[q, i], ends[i])
-
-    def far(q, i):
-        block = tok.at[q, Ys[2], parts[i]]
-        return remote(block, uhalf.at[q, i], b2_s.at[q, 2 + i], b2_r.at[q, 2 + i], ends[i])
-
-    def b1(q, i):
-        return remote(vout.at[q, As[i + 1]], vin.at[q, a], b1_s.at[q, i], b1_r.at[q, i], a_peers[i])
-
-    def load_up(q):
-        slot = q % 2
-        depth = pl.ds(pl.multiple_of(q * CW, CW), CW)
+            rows.at[u, 0, :, Cs[i + 1]], zin.at[u, c], b3_s.at[g, i], b3_r.at[g, i], c_peers[i]
+        )
+
+    def b2(g, i):
+        u = un(g, HOME)
+        return remote(tok.at[u, Yn[i]], uin.at[u, i], b2_s.at[g, i], b2_r.at[g, i], ends[i])
+
+    def far(g, i):
+        u = un(g, HOME)
+        block = tok.at[u, Ys[2], parts[i]]
+        return remote(block, uhalf.at[u, i], b2_s.at[g, 2 + i], b2_r.at[g, 2 + i], ends[i])
+
+    def b1(g, i):
+        u = un(g, HOME)
+        return remote(vout.at[u, As[i + 1]], vin.at[u, a], b1_s.at[g, i], b1_r.at[g, i], a_peers[i])
+
+    def units(g, body, groups=HOME):
+        q, n = groups[g]
+
+        def one(u, carry):
+            body(u)
+            return carry
+
+        if n == 1:
+            body(q)
+        else:
+            lax.fori_loop(q, q + n, one, 0)
+
+    def load_up(g):
+        q, n = OUT[g]
+        slot, depth, held = g % 2, pl.ds(q * CW, n * CW), pl.ds(0, n * CW)
         return (
-            pltpu.make_async_copy(wg_ref.at[:, depth], wgu.at[slot, :, :, 0:384], wg_m.at[slot]),
-            pltpu.make_async_copy(wu_ref.at[:, depth], wgu.at[slot, :, :, 384:768], wu_m.at[slot]),
+            pltpu.make_async_copy(wg_ref.at[:, depth], wgu.at[slot, :, held, 0:384], wg_m.at[slot]),
+            pltpu.make_async_copy(
+                wu_ref.at[:, depth], wgu.at[slot, :, held, 384:768], wu_m.at[slot]
+            ),
         )
 
     def load_down(q):
-        cols = pl.ds(pl.multiple_of(q * CW, CW), CW)
-        return pltpu.make_async_copy(wd_ref.at[:, :, cols], wdn.at[q % 3], wd_m.at[q % 3])
+        return pltpu.make_async_copy(
+            wd_ref.at[:, :, q * CW : (q + 1) * CW], wdn.at[q], wd_m.at[q]
+        )
 
     lane = lax.broadcasted_iota(jnp.int32, (32, 128), 1)
+    expert = (lane % 64).astype(F32)
+    same = lax.broadcasted_iota(jnp.int32, (32, 32), 0) == lax.broadcasted_iota(
+        jnp.int32, (32, 32), 1
+    )
+    turn = jnp.where(same, 1.0, 0.0).astype(BF)
+    across = (((1,), (1,)), ((), ()))
+    route_col = lax.dot_general(
+        turn, routes_ref[...].astype(F32).astype(BF), across, preferred_element_type=F32
+    )
+    gate_own = lax.dot_general(
+        turn, gates_ref[...].astype(BF), across, preferred_element_type=F32
+    )
     named = jnp.zeros((32, 128), F32)
     gate = jnp.zeros((32, 128), F32)
     for k in range(8):
-        hit = routes_ref[:, k : k + 1] == lane % 64
+        hit = route_col[:, k : k + 1] == expert
         named = named + jnp.where(hit, 1.0, 0.0)
-        gate = gate + jnp.where(hit, gates_ref[:, k : k + 1], 0.0)
+        gate = gate + jnp.where(hit, gate_own[:, k : k + 1], 0.0)
     before = (
         lax.broadcasted_iota(jnp.int32, (32, 32), 1) < lax.broadcasted_iota(jnp.int32, (32, 32), 0)
     )
@@ -374,34 +417,33 @@
         jnp.where(before, 1.0, 0.0).astype(BF), named.astype(BF), preferred_element_type=F32
     )
     meta[y, a] = jnp.where(lane < 64, jnp.where(named > 0.5, rank, -1.0), gate).astype(BF)
+    tok[:, y, a] = normed_ref[...]
+    for i in range(3):
+        s1(0, i).start()
     for i in range(3):
         m1(i).start()
-
-    def first(q, carry):
-        tok[q, y, a] = normed_ref[q]
-        for i in range(3):
-            s1(q, i).start()
-        return carry
-
-    lax.fori_loop(0, CH, first, 0)
-    for q in range(2):
-        for copy in load_up(q):
+    for g in range(2):
+        for copy in load_up(g):
             copy.start()
-    for q in range(3):
+    for q in range(CH):
         load_down(q).start()
+
+    def second(g):
+        for i in range(3):
+            s1(g, i).wait()
+        for i in range(2):
+            s2(g, i).start()
+
+    second(0)
+    for g in range(1, NO):
+        for i in range(3):
+            s1(g, i).start()
     for i in range(3):
         m1(i).wait()
     for i in range(3):
         m2(i).start()
-
-    def second(q):
-        for i in range(3):
-            s1(q, i).wait()
-        for i in range(2):
-            s2(q, i).start()
-
-    for q in range(AHEAD):
-        second(q)
+    for g in range(1, AHEAD):
+        second(g)
     for i in range(3):
         m2(i).wait()
 
@@ -439,149 +481,148 @@
         )
     give[...] = weight.astype(BF)
 
-    def pass_on(q):
-        for i in range(2):
-            s2(q, i).wait_recv()
-        for i in range(2):
-            relay(q, i).start()
-
-        @pl.when(q + AHEAD < CH)
-        def _():
-            second(q + AHEAD)
-
-    def select(q):
-        for i in range(2):
-            relay(q, i).wait_recv()
-
-        def one(o):
-            p = pick[lax.rem(c + o, 4)]
-            parts = [
-                jnp.dot(
-                    p,
-                    tok[q, :, :, :, n * 256 : (n + 1) * 256].reshape(512, 256),
-                    preferred_element_type=F32,
-                ).astype(BF).reshape(2, 96, 256)
-                for n in range(CW // 256)
-            ]
-            return parts
-
-        def other(i, carry):
-            for n, part in enumerate(one(i + 1)):
-                stage[q, i, :, :, n * 256 : (n + 1) * 256] = part
-            return carry
-
-        lax.fori_loop(0, 3, other, 0)
-        for i in range(3):
-            s3(q, i).start()
-        for n, part in enumerate(one(0)):
-            rows[q, 0, :, c, :, n * 256 : (n + 1) * 256] = part
-
-    def share(q):
-        for i in range(3):
-            s3(q, i).wait_recv()
-        s4(q).start()
-
-    def up(q):
-        for copy in load_up(q):
-            copy.wait()
-        s4(q).wait_recv()
-        slot = q % 2
-
-        def one(i, carry):
-            s, j = i // 2, i % 2
-            r = rows[q, s, j].reshape(384, CW)
+    def pass_on(g):
+        for i in range(2):
+            s2(g, i).wait_recv()
+        for i in range(2):
+            relay(g, i).start()
+        if g + AHEAD < NO:
+            second(g + AHEAD)
+
+    def chosen(q, o):
+        p = pick[lax.rem(c + o, 4)]
+        return [
+            jnp.dot(
+                p,
+                tok[q, :, :, :, n * 256 : (n + 1) * 256].reshape(512, 256),
+                preferred_element_type=F32,
+            ).astype(BF).reshape(2, 96, 256)
+            for n in range(CW // 256)
+        ]
+
+    def select(g):
+        for i in range(2):
+            relay(g, i).wait_recv()
+
+        def others(q):
+            def other(i, carry):
+                for n, part in enumerate(chosen(q, i + 1)):
+                    stage[q, i, :, :, n * 256 : (n + 1) * 256] = part
+                return carry
+
+            lax.fori_loop(0, 3, other, 0)
+
+        def own(q):
+            for n, part in enumerate(chosen(q, 0)):
+                rows[q, 0, :, c, :, n * 256 : (n + 1) * 256] = part
+
+        units(g, others, OUT)
+        for i in range(3):
+            s3(g, i).start()
+        units(g, own, OUT)
+
+    def share(g):
+        for i in range(3):
+            s3(g, i).wait_recv()
+        s4(g).start()
+
+    def up(g, s):
+        q, size = OUT[g]
+        slot = g % 2
+
+        def one(j, carry):
             for n in range(3):
                 cols = slice(n * 256, (n + 1) * 256)
-                d = jnp.dot(r, wgu[slot, j, :, cols], preferred_element_type=F32)
-                acc[s, j, :, cols] = acc[s, j, :, cols] + d
+                d = None if g == 0 else acc[s, j, :, cols]
+                for u in range(size):
+                    r = jnp.dot(
+                        rows[q + u, s, j].reshape(384, CW),
+                        wgu[slot, j, u * CW : (u + 1) * CW, cols],
+                        preferred_element_type=F32,
+                    )
+                    d = r if d is None else d + r
+                acc[s, j, :, cols] = d
             return carry
 
-        lax.fori_loop(0, 4, one, 0)
-
-        @pl.when(q < CH - 2)
-        def _():
-            for copy in load_up(q + 2):
-                copy.start()
-
-    acc[...] = jnp.zeros_like(acc)
-
-    def dispatch(step, carry):
-        @pl.when(step < CH)
-        def _():
+        lax.fori_loop(0, 2, one, 0)
+
+    for step in range(NO + 3):
+        if step < NO:
             pass_on(step)
-
-        @pl.when((step >= 1) & (step < CH + 1))
-        def _():
+        if 0 <= step - 1 < NO:
             select(step - 1)
-
-        @pl.when((step >= 2) & (step < CH + 2))
-        def _():
-            share(step - 2)
-
-        @pl.when(step >= 3)
-        def _():
-            up(step - 3)
-
-        return carry
-
-    lax.fori_loop(0, CH + 3, dispatch, 0)
-
-    def activate(i, carry):
-        s, j = i // 2, i % 2
-        v = acc[s, j, :, 0:384]
-        hid[s, j] = (v / (1.0 + jnp.exp(-v)) * acc[s, j, :, 384:768]).astype(BF)
-        return carry
-
-    lax.fori_loop(0, 4, activate, 0)
+        if 0 <= step - 3 < NO:
+            g = step - 3
+            s4(g).wait_recv()
+            up(g, 1)
+            if g + 2 < NO:
+                for copy in load_up(g + 2):
+                    copy.start()
+        if 0 <= step - 2 < NO:
+            g = step - 2
+            share(g)
+            for copy in load_up(g):
+                copy.wait()
+            up(g, 0)
+
+    def activate(s):
+        def one(j, carry):
+            v = acc[s, j, :, 0:384]
+            hid[s, j] = (v / (1.0 + jnp.exp(-v)) * acc[s, j, :, 384:768]).astype(BF)
+            return carry
+
+        lax.fori_loop(0, 2, one, 0)
 
     def down(q, s, j, n):
         return jnp.dot(
-            hid[s, j], wdn[lax.rem(q, 3), j, :, n * 256 : (n + 1) * 256], preferred_element_type=F32
-        )
-
-    def half(step, carry):
-        @pl.when(step < CH)
-        def _():
-            load_down(step).wait()
-
-            def one(j, carry):
-                for n in range(CW // 256):
-                    rows[step, 1, j, :, :, n * 256 : (n + 1) * 256] = (
-                        down(step, 1, j, n).astype(BF).reshape(4, 96, 256)
-                    )
-                return carry
-
-            lax.fori_loop(0, 2, one, 0)
+            hid[s, j], wdn[q, j, :, n * 256 : (n + 1) * 256], preferred_element_type=F32
+        )
+
+    def down_sibling(q):
+        def one(j, carry):
+            for n in range(CW // 256):
+                rows[q, 1, j, :, :, n * 256 : (n + 1) * 256] = (
+                    down(q, 1, j, n).astype(BF).reshape(4, 96, 256)
+                )
+            return carry
+
+        lax.fori_loop(0, 2, one, 0)
+
+    def down_own(q):
+        def one(j, carry):
+            for n in range(CW // 256):
+                cols = slice(n * 256, (n + 1) * 256)
+                v = down(q, 0, j, n).reshape(4, 96, 256) + back[q, j, :, :, cols].astype(F32)
+                rows[q, 0, j, :, :, cols] = v.astype(BF)
+            return carry
+
+        lax.fori_loop(0, 2, one, 0)
+        zin[q, c] = rows[q, 0, :, c]
+
+    activate(1)
+    for g in range(NO):
+        s4(g).wait_send()
+        for i in range(2):
+            s2(g, i).wait_send()
+            relay(g, i).wait_send()
+        for i in range(3):
+            s3(g, i).wait_send()
+    for step in range(NH + 1):
+        if step < NH:
+            q, n = HOME[step]
+            for u in range(q, q + n):
+                load_down(u).wait()
+            units(step, down_sibling)
             yb(step).start()
-
-        @pl.when(step >= 1)
-        def _():
-            q = step - 1
-            s4(q).wait_send()
-            yb(q).wait_recv()
-
-            def one(j, carry):
-                for n in range(CW // 256):
-                    cols = slice(n * 256, (n + 1) * 256)
-                    v = down(q, 0, j, n).reshape(4, 96, 256) + back[q, j, :, :, cols].astype(F32)
-                    rows[q, 0, j, :, :, cols] = v.astype(BF)
-                return carry
-
-            lax.fori_loop(0, 2, one, 0)
-            @pl.when(q < BACK)
-            def _():
+        if step == 0:
+            activate(0)
+        if step >= 1:
+            g = step - 1
+            yb(g).wait_recv()
+            units(g, down_own)
+            if g < BACK:
                 for i in range(3):
-                    b3(q, i).start()
-
-            zin[q, c] = rows[q, 0, :, c]
-
-            @pl.when(q < CH - 3)
-            def _():
-                load_down(q + 3).start()
-
-        return carry
-
-    lax.fori_loop(0, CH + 1, half, 0)
+                    b3(g, i).start()
 
     def one_sum(q, o):
         y_ = Ys[o]
@@ -592,80 +633,76 @@
                 g, zin[q, :, :, :, cols].reshape(768, 256), preferred_element_type=F32
             ).astype(BF).reshape(4, 32, 256)
 
-    def gather_sums(q):
-        for i in range(3):
-            b3(q, i).wait_recv()
-
-        @pl.when(q + BACK < CH)
-        def _():
+    def gather_sums(g):
+        for i in range(3):
+            b3(g, i).wait_recv()
+        if g + BACK < NH:
             for i in range(3):
-                b3(q + BACK, i).start()
-
-        for i in range(2):
-            s2(q, i).wait_send()
-            relay(q, i).wait_send()
-        one_sum(q, 2)
-        for i in range(2):
-            far(q, i).start()
-        for o in (1, 3, 0):
-            one_sum(q, o)
-
-    def add_half(q):
-        for i in range(2):
-            far(q, i).wait_recv()
-            block = tok[q, Yn[i], parts[i]].astype(F32) + uhalf[q, i].astype(F32)
-            tok[q, Yn[i], parts[i]] = block.astype(BF)
-            b2(q, i).start()
-
-    def along(q):
-        for i in range(2):
-            b2(q, i).wait_recv()
-        v = uin[q, 0].astype(F32) + uin[q, 1].astype(F32) + tok[q, y].astype(F32)
-        vout[q] = v.astype(BF)
-        for i in range(3):
-            b1(q, i).start()
-        vin[q, a] = vout[q, a]
-
-    def store(q):
-        for i in range(3):
-            b1(q, i).wait_recv()
-        v = vin[q, 0].astype(F32) + vin[q, 1].astype(F32)
-        v = v + vin[q, 2].astype(F32) + vin[q, 3].astype(F32)
-        out_ref[:, pl.ds(pl.multiple_of(q * CW, CW), CW)] = (hsum_ref[q] + v).astype(BF)
-
-    def combine(step, carry):
-        @pl.when((step >= 1) & (step < CH + 1))
-        def _():
+                b3(g + BACK, i).start()
+        units(g, lambda q: one_sum(q, 2))
+        for i in range(2):
+            far(g, i).start()
+
+        def rest(q):
+            for o in (1, 3, 0):
+                one_sum(q, o)
+
+        units(g, rest)
+
+    def add_half(g):
+        for i in range(2):
+            far(g, i).wait_recv()
+
+            def add(q):
+                block = tok[q, Yn[i], parts[i]].astype(F32) + uhalf[q, i].astype(F32)
+                tok[q, Yn[i], parts[i]] = block.astype(BF)
+
+            units(g, add)
+            b2(g, i).start()
+
+    def along(g):
+        for i in range(2):
+            b2(g, i).wait_recv()
+
+        def add(q):
+            v = uin[q, 0].astype(F32) + uin[q, 1].astype(F32) + tok[q, y].astype(F32)
+            vout[q] = v.astype(BF)
+            vin[q, a] = vout[q, a]
+
+        units(g, add)
+        for i in range(3):
+            b1(g, i).start()
+
+    def store(g):
+        for i in range(3):
+            b1(g, i).wait_recv()
+
+        def add(q):
+            v = vin[q, 0].astype(F32) + vin[q, 1].astype(F32)
+            v = v + vin[q, 2].astype(F32) + vin[q, 3].astype(F32)
+            cols = pl.ds(pl.multiple_of(q * CW, CW), CW)
+            out_ref[:, cols] = (hsum_ref[q] + v).astype(BF)
+
+        units(g, add)
+
+    for step in range(NH + 3):
+        if 0 <= step - 1 < NH:
             add_half(step - 1)
-
-        @pl.when(step < CH)
-        def _():
+        if step < NH:
             gather_sums(step)
-
-        @pl.when((step >= 2) & (step < CH + 2))
-        def _():
+        if 0 <= step - 2 < NH:
             along(step - 2)
-
-        @pl.when(step >= 3)
-        def _():
+        if 0 <= step - 3 < NH:
             store(step - 3)
 
-        return carry
-
-    lax.fori_loop(0, CH + 3, combine, 0)
-
-    def finish(q, carry):
-        yb(q).wait_send()
-        for i in range(3):
-            s3(q, i).wait_send()
-            b3(q, i).wait_send()
-            b1(q, i).wait_send()
-        for i in range(2):
-            far(q, i).wait_send()
-            b2(q, i).wait_send()
-        return carry
-
-    lax.fori_loop(0, CH, finish, 0)
+    for g in range(NH):
+        yb(g).wait_send()
+        for i in range(3):
+            b3(g, i).wait_send()
+            b1(g, i).wait_send()
+        for i in range(2):
+            far(g, i).wait_send()
+            b2(g, i).wait_send()
 
 
 def mixture(normed, hsum, routes, gates, w_gate, w_up, w_down):
@@ -684,8 +721,8 @@
             pltpu.VMEM((CH, 2, 2, 4, 96, CW), BF),
             pltpu.VMEM((2, 2, 384, 768), F32),
             pltpu.VMEM((2, 2, 384, 384), BF),
-            pltpu.VMEM((2, 2, CW, 768), BF),
-            pltpu.VMEM((3, 2, 384, CW), BF),
+            pltpu.VMEM((2, 2, 2 * CW, 768), BF),
+            pltpu.VMEM((CH, 2, 384, CW), BF),
             pltpu.VMEM((CH, 2, 4, 96, CW), BF),
             pltpu.VMEM((CH, 4, 2, 96, CW), BF),
             pltpu.VMEM((CH, 2, 4, 32, CW), BF),
@@ -695,10 +732,10 @@
             pltpu.VMEM((4, 192, 512), BF),
             pltpu.VMEM((512, 768), BF),
             dma((6,)), dma((6,)),
-            dma((CH, 3)), dma((CH, 3)), dma((CH, 4)), dma((CH, 4)), dma((CH, 3)), dma((CH, 3)),
-            dma((CH,)), dma((CH,)), dma((CH,)), dma((CH,)),
-            dma((CH, 3)), dma((CH, 3)), dma((CH, 4)), dma((CH, 4)), dma((CH, 3)), dma((CH, 3)),
-            dma((2,)), dma((2,)), dma((3,)),
+            dma((NO, 3)), dma((NO, 3)), dma((NO, 4)), dma((NO, 4)), dma((NO, 3)), dma((NO, 3)),
+            dma((NO,)), dma((NO,)), dma((NH,)), dma((NH,)),
+            dma((NH, 3)), dma((NH, 3)), dma((NH, 4)), dma((NH, 4)), dma((NH, 3)), dma((NH, 3)),
+            dma((2,)), dma((2,)), dma((CH,)),
         ],
         compiler_params=pltpu.CompilerParams(
             collective_id=1, has_side_effects=True, vmem_limit_bytes=63 * 2**20
@@ -706,7 +743,7 @@
         cost_estimate=pl.CostEstimate(
             flops=20 * 10**9, bytes_accessed=20 * 2**20, transcendentals=2**20
         ),
-    )(normed, hsum, routes, gates, w_gate, w_up, w_down)
+    )(normed, hsum, routes.T, gates.T, w_gate, w_up, w_down)
 
 
 def shards(

time: 217 us -> 209 us (0.963)
  Pallas kernels: 212 us -> 207 us
  local copies, waits for them, and re-layouts: 4.39 us -> 1.67 us
    pallas_call x1, Pallas kernels: 137 us -> 131 us  [mixture(): pl.pallas_call(experts_kernel, out_shape=jax.ShapeDtypeStruct((32, D), BF...]
    unnamed x3 -> x1, local copies, waits for them, and re-layouts: 4.39 us -> 1.67 us
where the time goes in v4:
time: 209 us
  Pallas kernels  207 us (99%)
    pallas_call x1, Pallas kernels, mixture(): pl.pallas_call(experts_kernel, out_shape=jax.ShapeDtypeStruct((32, D), BF...  131 us
    pallas_call x1, Pallas kernels, attention(): pl.pallas_call(attention_kernel, out_shape=(jax.ShapeDtypeStruct((8, 32,...  75.8 us

profile of v4, /device:TPU:0, one launch (start us, length us, event | category | flops | bytes accessed | tf_op | source)
XLA Modules:
  0.0 208.9 jit_solution(3720724232922825887)
XLA Ops:
  0.0 75.8 %shard_map.109 = (f32[8,32,512]{2,1,0:T(8,128)}, bf16[8,32,512]{2,1,0:T(8,128)(2,1)}) custom-call(bf16[128,2048]{1,0:T(8,128)(2,1)} %q_ref.1, bf16[128,128]{1,0:T(8,128)(2,1)} %k_ref.1, bf16[128,128]{1,0:T(8,128)(2,1)} %v_ref.1, bf16[2048,128]{1,0:T(8,128)(2,1)} %w_ref.1, bf16[32,4096]{1,0:T(8,128)(2,1)} %resid_ref.1, f32[1,4096]{1,0:T(1,128)} %bitcast.3), custom_call_target="tpu_custom_call" | custom-call | flops 8000000000 | bytes 4194304 | tf_op jit(solution)/shard_map/pallas_call | solution.py:241
  75.8 131.4 %shard_map.110 = bf16[32,4096]{1,0:T(8,128)(2,1)} custom-call(bf16[8,32,512]{2,1,0:T(8,128)(2,1)} %get-tuple-element.7.normed_ref, f32[8,32,512]{2,1,0:T(8,128)} %get-tuple-element.8.hsum_ref, s32[8,32]{1,0:T(8,128)} %bitcast.4, f32[8,32]{1,0:T(8,128)} %bitcast.5, bf16[2,4096,384]{2,1,0:T(8,128)(2,1)} %wg_ref.1, bf16[2,4096,384]{2,1,0:T(8,128)(2,1)} %wu_ref.1, ...), custom_call_target="tpu_custom_call" | custom-call | flops 20000000000 | bytes 20971520 | tf_op jit(solution)/shard_map/pallas_call | solution.py:712
  207.2 1.7 copy.13

commit v5 on v4

--- a/solution.py
+++ b/solution.py
@@ -60,7 +60,7 @@
     me = (z, x, yl)
     mine = pl.ds(pl.multiple_of((x * 2 + yl) * 128, 128), 128)
     both = pl.ds(pl.multiple_of(x * 256, 256), 256)
-    low, high = pl.ds(0, 1024), pl.ds(1024, 1024)
+    low, high = pl.ds(0, 896), pl.ds(896, 1152)
     wall[:, mine] = w_ref[...]
 
     def wa1():
@@ -107,11 +107,7 @@
         k2[i].wait_recv()
         k_on(1 + i, x_)
     w1 = wb1() + wa1()
-    w1[3].wait_recv()
-    w2 = [
-        send(wall.at[low, both], wall.at[low, both], w_s.at[4 + i], w_r.at[4 + i], x_peers[i])
-        for i in range(3)
-    ]
+    w2 = []
 
     def wb2(p, x_):
         cols = pl.ds(pl.multiple_of((x_ * 2 + yl) * 128, 128), 128)
@@ -125,6 +121,13 @@
         for i in range(3):
             w1[i].wait_recv()
             wb2(1 + i, lax.rem(x + 3 - i, 4))
+        w1[3].wait_recv()
+        for i in range(3):
+            w2.append(
+                send(
+                    wall.at[low, both], wall.at[low, both], w_s.at[4 + i], w_r.at[4 + i], x_peers[i]
+                )
+            )
 
     factor = HW**-0.5 * 1.4426950408889634
     last = ctx // 4

time: 209 us -> 207 us (level)
  no operation moved by 1% of the time
where the time goes in v5:
time: 207 us
  Pallas kernels  205 us (99%)
    pallas_call x1, Pallas kernels, mixture(): pl.pallas_call(experts_kernel, out_shape=jax.ShapeDtypeStruct((32, D), BF...  130 us
    pallas_call x1, Pallas kernels, attention(): pl.pallas_call(attention_kernel, out_shape=(jax.ShapeDtypeStruct((8, 32,...  75.1 us

profile of v5, /device:TPU:0, one launch (start us, length us, event | category | flops | bytes accessed | tf_op | source)
XLA Modules:
  0.0 207.1 jit_solution(2739657850159579705)
XLA Ops:
  0.0 75.1 %shard_map.109 = (f32[8,32,512]{2,1,0:T(8,128)}, bf16[8,32,512]{2,1,0:T(8,128)(2,1)}) custom-call(bf16[128,2048]{1,0:T(8,128)(2,1)} %q_ref.1, bf16[128,128]{1,0:T(8,128)(2,1)} %k_ref.1, bf16[128,128]{1,0:T(8,128)(2,1)} %v_ref.1, bf16[2048,128]{1,0:T(8,128)(2,1)} %w_ref.1, bf16[32,4096]{1,0:T(8,128)(2,1)} %resid_ref.1, f32[1,4096]{1,0:T(1,128)} %bitcast.3), custom_call_target="tpu_custom_call" | custom-call | flops 8000000000 | bytes 4194304 | tf_op jit(solution)/shard_map/pallas_call | solution.py:244
  75.1 130.3 %shard_map.110 = bf16[32,4096]{1,0:T(8,128)(2,1)} custom-call(bf16[8,32,512]{2,1,0:T(8,128)(2,1)} %get-tuple-element.7.normed_ref, f32[8,32,512]{2,1,0:T(8,128)} %get-tuple-element.8.hsum_ref, s32[8,32]{1,0:T(8,128)} %bitcast.4, f32[8,32]{1,0:T(8,128)} %bitcast.5, bf16[2,4096,384]{2,1,0:T(8,128)(2,1)} %wg_ref.1, bf16[2,4096,384]{2,1,0:T(8,128)(2,1)} %wu_ref.1, ...), custom_call_target="tpu_custom_call" | custom-call | flops 20000000000 | bytes 20971520 | tf_op jit(solution)/shard_map/pallas_call | solution.py:715
  205.4 1.7 copy.13
